TPU v7x, 256 devices: a whole 4x4x8 slice. The times are simulated.
256 devices in a mesh: gx: 8 (over z), gy: 32 (over y, x, core).
Axes of the slice: x: 4, y: 4, z: 8, core: 2. Of those that a mesh axis runs over, the one named last changes fastest.
Arguments:
- reference_scan: bfloat16 [256, 1024, 128], P('gx', 'gy'), may hold values from -6 to 6
- deformed_scan: bfloat16 [256, 1024, 128], P('gx', 'gy'), may hold values from -6 to 6
- source_column: int32 [8, 32, 64, 1], P('gx'), may hold values from 0 to 31, as said below
Outputs:
- update: float32 [3, 16, 64, 9], P(None, 'gx', 'gy')
- cg_residual: float32 [3, 16, 64, 9], P(None, 'gx', 'gy')
Inputs may be any that keep to these rules, and one draw needn't show every extreme that they name: source_column[p, q, b, 0] is q - 1, q or q + 1. Within one brick's 64 blocks at most 16 come from column q - 1 and at most 16 from column q + 1; in every draw some brick takes exactly 16 blocks from column q - 1 and some brick exactly 16 from column q + 1.
All inputs are finite; a program needn't handle non-finite values.
Results may differ from a plain program's by a relative error of at most 0.0003.
Values may be sent and summed in bfloat16 or wider, within the bound.
A program may use at most 64 MiB of HBM per device.

v0:
```python
import jax
import jax.numpy as jnp
from jax import lax
from jax.sharding import PartitionSpec as P

E = 16
ITERS = 4


damping = 0.1


def extended(cells, sides, width):
    for axis, dim in sides:
        count = lax.axis_size(axis)
        ends = count - 1
        head = lax.slice_in_dim(cells, 0, width, axis=dim)
        tail = lax.slice_in_dim(cells, cells.shape[dim] - width, cells.shape[dim], axis=dim)
        cells = jnp.concatenate(
            [
                lax.ppermute(tail, axis, [(i, (i + 1) % count) for i in range(ends)]),
                cells,
                lax.ppermute(head, axis, [((i + 1) % count, i) for i in range(ends)]),
            ],
            axis=dim,
        )
    return cells


def passed_along(value, axis, steps):
    count = lax.axis_size(axis)
    leading, last = (max(0, -steps), min(count, count - steps))
    return lax.ppermute(value, axis, [(source, source + steps) for source in range(leading, last)])


def shape_matrix(count, nodes, edge):
    position = jnp.arange(count, dtype=jnp.float32)[:, None]
    anchor = jnp.arange(nodes, dtype=jnp.float32)[None, :] * edge
    return jnp.maximum(0.0, 1.0 - jnp.abs(position - anchor) / edge)


def to_blocks(brick):
    first, second, third = brick.shape
    pieces = brick.reshape(first // 8, 8, second // 8, 8, 4, third // 4)
    return pieces.transpose(0, 2, 4, 1, 3, 5).reshape(-1, 16 * third)


def from_blocks(blocks, first, second, third):
    pieces = blocks.reshape(first // 8, second // 8, 4, 8, 8, third // 4)
    return pieces.transpose(0, 3, 1, 4, 2, 5).reshape(first, second, third)


def inner(left, right):
    return jnp.sum(left * right)


def squares(residual):
    return lax.psum(inner(residual, residual), ("gx", "gy"))


def local(reference_scan, deformed_scan, source_column):
    cells_first, cells_second, cells_third = reference_scan.shape
    own_blocks = to_blocks(deformed_scan)
    table = source_column[0, :, :, 0]
    column = lax.axis_index("gy")
    wanted = lax.dynamic_index_in_dim(table, column, 0, keepdims=False)
    widened = extended(deformed_scan, (("gy", 1),), cells_second)
    lower_blocks = to_blocks(widened[:, :cells_second])
    upper_blocks = to_blocks(widened[:, 2 * cells_second :])
    offset = (wanted - column)[:, None]
    fetched = jnp.where(
        offset < 0, lower_blocks, jnp.where(offset > 0, upper_blocks, own_blocks)
    ).astype(jnp.float32)
    warped = from_blocks(fetched, cells_first, cells_second, cells_third)
    rimmed = extended(reference_scan, (("gx", 0), ("gy", 1)), 1)
    padded = jnp.pad(rimmed.astype(jnp.float32), ((0, 0), (0, 0), (1, 1)))
    scale = 1.0 / (2.0 * E)
    gradient = jnp.stack(
        [
            (padded[2:, 1:-1, 1:-1] - padded[:-2, 1:-1, 1:-1]) * scale,
            (padded[1:-1, 2:, 1:-1] - padded[1:-1, :-2, 1:-1]) * scale,
            (padded[1:-1, 1:-1, 2:] - padded[1:-1, 1:-1, :-2]) * scale,
        ]
    )
    misfit = padded[1:-1, 1:-1, 1:-1] - warped
    nodes_first = cells_first // E
    nodes_second = cells_second // E
    nodes_third = cells_third // E + 1
    matrix_x = shape_matrix(cells_first, nodes_first + 1, float(E))
    matrix_y = shape_matrix(cells_second, nodes_second + 1, float(E))
    matrix_z = shape_matrix(cells_third, nodes_third, float(E))
    highest = lax.Precision.HIGHEST

    def fold_back(voxels):
        temp = jnp.einsum("cxyz,xi->ciyz", voxels, matrix_x, precision=highest)
        temp = jnp.einsum("ciyz,yj->cijz", temp, matrix_y, precision=highest)
        nodal = jnp.einsum("cijz,zk->cijk", temp, matrix_z, precision=highest)
        lower_y = passed_along(nodal[:, :, -1], "gy", 1)
        nodal = nodal[:, :, :-1].at[:, :, 0].add(lower_y)
        lower_x = passed_along(nodal[:, -1], "gx", 1)
        return nodal[:, :-1].at[:, 0].add(lower_x)

    rhs = fold_back(gradient * misfit[None])
    update = jnp.zeros_like(rhs)
    residual = rhs
    direction = rhs
    norm_now = squares(residual)
    for turn in range(ITERS):
        upper_x = passed_along(direction[:, 0], "gx", -1)
        wider = jnp.concatenate([direction, upper_x[:, None]], axis=1)
        upper_y = passed_along(wider[:, :, 0], "gy", -1)
        spread_temp = jnp.einsum(
            "cijk,zk->cijz",
            jnp.concatenate([wider, upper_y[:, :, None]], axis=2),
            matrix_z,
            precision=highest,
        )
        spread_temp = jnp.einsum("cijz,yj->ciyz", spread_temp, matrix_y, precision=highest)
        moved = jnp.einsum("ciyz,xi->cxyz", spread_temp, matrix_x, precision=highest)
        along = jnp.sum(gradient * moved, axis=0)
        image = fold_back(gradient * along[None]) + damping * direction
        alpha = norm_now / lax.psum(inner(direction, image), ("gx", "gy"))
        update = update + alpha * direction
        residual = residual - alpha * image
        norm_next = squares(residual)
        direction = residual + norm_next / norm_now * direction
        norm_now = norm_next
    return (update, residual)


def solution(mesh):
    return jax.shard_map(
        local,
        mesh=mesh,
        in_specs=(P("gx", "gy", None), P("gx", "gy", None), P("gx", None, None, None)),
        out_specs=(P(None, "gx", "gy", None), P(None, "gx", "gy", None)),
        check_vma=False,
    )
```

profile of v0, /device:TPU:1, one launch (start us, length us, event | category | flops | bytes accessed | tf_op | source)
XLA Modules:
  0.0 690.3 jit_solution(11465054970750083549)
XLA Ops:
  0.6 4.5 collective-permute-start.4
  9.1 4.1 collective-permute-start
  15.1 4.6 collective-permute-start.2
  28.1 3.6 collective-permute-start.6
  32.5 3.9 collective-permute-start.7
  38.5 3.3 collective-permute-done.8
  41.8 2.8 collective-permute-start.9
  44.5 4.8 collective-permute-done.9
  58.0 4.0 collective-permute-start.11
  63.4 89.8 %all-reduce.1 = (f32[]{:T(128)}, f32[]{:T(128)}) all-reduce(f32[]{:T(128)} %get-tuple-element.125, f32[]{:T(128)} %get-tuple-element.124), channel_id=1, replica_groups=mesh['gx'=8,'gy'=32] {'gx','gy'}, use_global_device_ids=true, to_apply=%region_1.2 | all-reduce | flops 2 | bytes 16 | tf_op jit(solution)/shard_map/psum | solution.py:58
  155.1 74.4 %psum.58 = f32[]{:T(128)} all-reduce(f32[]{:T(128)} %multiply_reduce_fusion.5), channel_id=1, replica_groups=mesh['gx'=8,'gy'=32] {'gx','gy'}, use_global_device_ids=true, to_apply=%region_6.7 | all-reduce | flops 1 | bytes 8 | tf_op jit(solution)/shard_map/psum | solution.py:58
  232.2 3.0 collective-permute-done.12
  235.2 3.7 collective-permute-start.13
  252.2 80.1 %psum.59 = f32[]{:T(128)} all-reduce(f32[]{:T(128)} %multiply_reduce_fusion.4), channel_id=1, replica_groups=mesh['gx'=8,'gy'=32] {'gx','gy'}, use_global_device_ids=true, to_apply=%region_9.10 | all-reduce | flops 1 | bytes 8 | tf_op jit(solution)/shard_map/psum | solution.py:122
  334.2 73.3 %psum.60 = f32[]{:T(128)} all-reduce(f32[]{:T(128)} %get-tuple-element.130), channel_id=1, replica_groups=mesh['gx'=8,'gy'=32] {'gx','gy'}, use_global_device_ids=true, to_apply=%region_11.12 | all-reduce | flops 1 | bytes 8 | tf_op jit(solution)/shard_map/psum | solution.py:58
  410.2 3.0 collective-permute-done.16
  413.3 3.9 collective-permute-start.17
  427.3 2.9 collective-permute-start.19
  431.5 78.8 %psum.61 = f32[]{:T(128)} all-reduce(f32[]{:T(128)} %multiply_reduce_fusion.2), channel_id=1, replica_groups=mesh['gx'=8,'gy'=32] {'gx','gy'}, use_global_device_ids=true, to_apply=%region_14.15 | all-reduce | flops 1 | bytes 8 | tf_op jit(solution)/shard_map/psum | solution.py:122
  512.3 73.3 %psum.62 = f32[]{:T(128)} all-reduce(f32[]{:T(128)} %get-tuple-element.128), channel_id=1, replica_groups=mesh['gx'=8,'gy'=32] {'gx','gy'}, use_global_device_ids=true, to_apply=%region_16.17 | all-reduce | flops 1 | bytes 8 | tf_op jit(solution)/shard_map/psum | solution.py:58
  588.3 3.0 collective-permute-done.20
  591.3 3.7 collective-permute-start.21
  605.3 2.9 collective-permute-start.23
  609.6 78.8 %psum.63 = f32[]{:T(128)} all-reduce(f32[]{:T(128)} %multiply_reduce_fusion), channel_id=1, replica_groups=mesh['gx'=8,'gy'=32] {'gx','gy'}, use_global_device_ids=true, to_apply=%region_19.20 | all-reduce | flops 1 | bytes 8 | tf_op jit(solution)/shard_map/psum | solution.py:122
  (151 shorter events, 69.1 us)
Async XLA Ops:
  0.6 24.3 %collective-permute-start.4 = (bf16[32,32,128]{2,1,0:T(8,128)(2,1)}, bf16[32,32,128]{2,1,0:T(8,128)(2,1)S(1)}, u32[]{:S(2)}, u32[]{:S(2)}) collective-permute-start(bf16[32,32,128]{2,1,0:T(8,128)(2,1)} %param.24), channel_id=1, source_target_pairs={{0,1},{1,2},{2,3},{3,4},{4,5},{5,6},{6,7},{7,8},{8,9},{9,10},{10,1... | collective-permute-start | bytes 786440 | tf_op jit(solution)/shard_map/ppermute | solution.py:21
  5.1 19.8 %collective-permute-start.5 = (bf16[32,32,128]{2,1,0:T(8,128)(2,1)}, bf16[32,32,128]{2,1,0:T(8,128)(2,1)S(1)}, u32[]{:S(2)}, u32[]{:S(2)}) collective-permute-start(bf16[32,32,128]{2,1,0:T(8,128)(2,1)} %param.24), channel_id=1, source_target_pairs={{1,0},{2,1},{3,2},{4,3},{5,4},{6,5},{7,6},{8,7},{9,8},{10,9},{11,1... | collective-permute-start | bytes 786440 | tf_op jit(solution)/shard_map/ppermute | solution.py:23
  7.8 7.2 %collective-permute-start.1 = (bf16[1,32,128]{2,1,0:T(8,128)(2,1)S(1)}, bf16[1,32,128]{2,1,0:T(8,128)(2,1)S(1)}, u32[]{:S(2)}, u32[]{:S(2)}) collective-permute-start(bf16[1,32,128]{2,1,0:T(8,128)(2,1)S(1)} %get-tuple-element.138), channel_id=1, source_target_pairs={{32,0},{64,32},{96,64},{128,96},{160,128},{192,160},{224,192},{33,... | collective-permute-start | bytes 24584 | tf_op jit(solution)/shard_map/ppermute | solution.py:23
  9.1 4.9 collective-permute-start
  15.1 9.7 %collective-permute-start.2 = (bf16[34,1,128]{2,1,0:T(2,128)(2,1)S(1)}, bf16[34,1,128]{2,1,0:T(2,128)(2,1)S(1)}, u32[]{:S(2)}, u32[]{:S(2)}) collective-permute-start(bf16[34,1,128]{2,1,0:T(2,128)(2,1)S(1)} %get-tuple-element.136), channel_id=1, source_target_pairs={{0,1},{1,2},{2,3},{3,4},{4,5},{5,6},{6,7},{7,8},{8,9},{9,10},{10,1... | collective-permute-start | bytes 26120 | tf_op jit(solution)/shard_map/ppermute | solution.py:21
  19.7 5.1 collective-permute-start.3
  28.1 4.4 collective-permute-start.6
  32.5 4.6 collective-permute-start.7
  37.2 4.6 collective-permute-start.8
  41.8 7.5 %collective-permute-start.9 = (f32[3,3,9]{2,1,0:T(4,128)S(1)}, f32[3,3,9]{2,1,0:T(4,128)S(1)}, u32[]{:S(2)}, u32[]{:S(2)}) collective-permute-start(f32[3,3,9]{2,1,0:T(4,128)S(1)} %bitcast.237), channel_id=1, source_target_pairs={{1,0},{2,1},{3,2},{4,3},{5,4},{6,5},{7,6},{8,7},{9,8},{10,9},{11,1... | collective-permute-start | bytes 980 | tf_op jit(solution)/shard_map/ppermute | solution.py:33
  54.8 3.1 collective-permute-start.10
  58.0 4.8 collective-permute-start.11
  230.9 4.3 collective-permute-start.12
  235.2 5.3 collective-permute-start.13
  246.0 3.1 collective-permute-start.14
  249.2 2.4 collective-permute-start.15
  408.9 4.3 collective-permute-start.16
  413.3 5.3 collective-permute-start.17
  424.2 3.1 collective-permute-start.18
  427.3 3.6 collective-permute-start.19
  587.0 4.3 collective-permute-start.20
  591.3 5.3 collective-permute-start.21
  602.2 3.1 collective-permute-start.22
  605.3 3.6 collective-permute-start.23
  (1 other events, 2.4 us)
where the time goes:
time: 692 us; the launch traced here: 690 us
  blocking collectives  549 us (79%)
  starting transfers between devices  64.4 us (9%)
  waiting for transfers between devices  31.2 us (5%)
  matrix products  18.5 us (3%)
  other arithmetic  12.3 us (2%)
  between operations  10.8 us (2%)
    psum x4, blocking collectives, squares(): return lax.psum(inner(residual, residual), ('gx', 'gy'))  311 us
    psum x3, blocking collectives, local(): alpha = norm_now / lax.psum(inner(direction, image), ('gx', 'gy'))  238 us
    ppermute x18, starting transfers between devices, passed_along(): lax.ppermute(value, axis, [(source, source + steps) for source in range(l...  46 us
    ppermute x18, waiting for transfers between devices, passed_along(): lax.ppermute(value, axis, [(source, source + steps) for source in range(l...  30.4 us
  transfers between devices with their start and end apart: 24, of which 19 were waited for; matrix products, arithmetic and copies ran while one was open for 1% of the time, Pallas kernels for 0%

commit v1 on v0

v1 whole, which is shorter than its diff:
```python
import functools

import jax
import jax.numpy as jnp
import ml_dtypes
import numpy as np
from jax import lax
from jax.experimental import pallas as pl
from jax.experimental.pallas import tpu as pltpu
from jax.sharding import PartitionSpec as P

MESH = pl.DeviceIdType.MESH
E = 16
ITERS = 4
DAMPING = 0.1
NGX, NGY = 8, 32
F32, BF16 = jnp.float32, jnp.bfloat16

NEIGHBOURS = [(dx, dy) for dx in (-1, 0, 1) for dy in (-1, 0, 1) if (dx, dy) != (0, 0)]
SOURCES = [(bx, by) for bx in (-2, -1, 0, 1) for by in (-2, -1, 0, 1) if (bx, by) != (0, 0)]
PAIRS = [(0, 0), (1, 1), (2, 2), (0, 1), (1, 2), (2, 0)]


def hat(position):
    return np.maximum(0.0, 1.0 - np.abs(position) / E)


def chain(count, nodes):
    position = np.arange(count)
    w = np.stack([hat(position - E * n) for n in range(nodes)])
    out = []
    for n in range(nodes):
        out.append(w[n] * w[n])
        if n + 1 < nodes:
            out.append(w[n] * w[n + 1])
    return w, np.stack(out)


def constants():
    wy, cy = chain(32, 3)
    wz, cz = chain(128, 9)
    scale = 1.0 / 1024.0
    ymat = np.zeros((48, 192))
    for m in range(5):
        for p in range(6):
            ymat[m * 8 + p, p * 32 : (p + 1) * 32] = cy[m] * scale
    zd, zf = np.zeros((128, 16)), np.zeros((128, 16))
    zd[:, :9] = cz[0::2].T
    zf[:, :8] = cz[1::2].T
    wmat = np.zeros((5, 128, 4, 8, 16))
    D0, F0, D1, F1, D2 = range(5)
    place = {
        (0, 0): (F0, zd), (0, 1): (F1, zd), (0, 2): (D1, zd), (0, 3): (D2, zd),
        (0, 4): (F0, zf), (0, 5): (F1, zf), (0, 6): (D1, zf), (0, 7): (D2, zf),
        (1, 2): (D0, zd), (1, 3): (D1, zd), (1, 4): (D2, zd), (1, 5): (F0, zd), (1, 6): (F1, zd),
        (2, 2): (D0, zf), (2, 3): (D1, zf), (2, 4): (D2, zf), (2, 5): (F0, zf), (2, 6): (F1, zf),
        (3, 4): (D0, zd), (3, 5): (F0, zd), (3, 6): (D0, zf), (3, 7): (F0, zf),
    }
    for (group, block), (m, z) in place.items():
        wmat[m, :, group, block, :] = z
    wmat = wmat.reshape(640, 512)
    yr = np.zeros((32, 96))
    for n in range(3):
        for r in range(8):
            c = r % 3
            yr[n * 8 + r, c * 32 : (c + 1) * 32] = wy[n] / 32.0
    wr = np.zeros((3, 128, 8, 16))
    for n in range(3):
        wr[n, :, 2 + n, :9] = wz.T
    wr = wr.reshape(384, 128)
    dz = np.zeros((128, 128))
    for z in range(128):
        if z + 1 < 128:
            dz[z + 1, z] = 1.0
        if z > 0:
            dz[z - 1, z] = -1.0
    lanes = np.arange(128)
    spread = (np.arange(64)[:, None] % 4 == lanes[None, :] // 32).astype(np.float64)
    small = np.zeros((256, 256))
    cast = lambda a: a.astype(ml_dtypes.bfloat16)
    return [cast(a) for a in (ymat, wmat, yr, wr, dz, spread)]


def pieces(x):
    hi = x.astype(BF16)
    rest = x - hi.astype(F32)
    mid = rest.astype(BF16)
    low = (rest - mid.astype(F32)).astype(BF16)
    return hi, mid, low


def mm(a, b):
    return jnp.dot(a, b, preferred_element_type=F32)


def kernel(
    ref_h, def_h, table, ymat, wmat_h, yr, wr, dz, spread,
    upd_out, res_out,
    ref_v, own_v, lo_v, hi_v, fs, gs, mask_s, yface, xlo, xhi, ylo, yhi,
    xs, t2, ksend, krecv, rx, rt2, rsend, rrecv, kf, wmat, vsend, vrecv,
    asrc, a1, b1src, b1, asrc2, a2, b2src, b2,
    lsem, fsend, frecv, ksem_s, ksem_r, rsem_s, rsem_r, vsem_s, vsem_r, arsem_s, arsem_r,
):
    gx, gy = lax.axis_index("gx"), lax.axis_index("gy")

    def at(dx, dy):
        return (lax.rem(gx + (dx + NGX), NGX), lax.rem(gy + (dy + NGY), NGY))

    barrier = pltpu.get_barrier_semaphore()
    partners = [at(0, m) for m in range(1, NGY)] + [at(m, 0) for m in range(1, NGX)]
    partners += [at(bx, by) for bx, by in SOURCES if bx != 0 and by != 0]
    for partner in partners:
        pl.semaphore_signal(barrier, inc=1, device_id=partner, device_id_type=MESH)

    load_ref = pltpu.make_async_copy(ref_h, ref_v, lsem.at[0])
    load_own = pltpu.make_async_copy(def_h, own_v, lsem.at[1])
    load_w = pltpu.make_async_copy(wmat_h, wmat, lsem.at[2])
    load_ref.start()
    load_own.start()
    load_w.start()

    def flag(condition):
        return jnp.where(condition, 1.0, 0.0).astype(F32)

    xlo_ok, xhi_ok = flag(gx > 0), flag(gx < NGX - 1)
    ylo_ok, yhi_ok = flag(gy > 0), flag(gy < NGY - 1)

    row = (table[gy] - gy).astype(F32)
    r16 = lax.broadcasted_iota(jnp.int32, (16, 64), 0)
    c64 = lax.broadcasted_iota(jnp.int32, (16, 64), 1)
    picked = jnp.where(c64 // 4 == r16, jnp.broadcast_to(row, (16, 64)), 0.0).astype(BF16)
    mask_s[...] = mm(picked, spread[...])

    load_ref.wait()
    for x in range(32):
        plane = ref_v[x]
        fs[x + 1, 8:40, :] = plane.astype(F32)
        gs[2, x] = mm(plane, dz[...])
    yface[0] = jnp.concatenate([fs[x + 1, 39:40, :] for x in range(32)], axis=0).astype(BF16)
    yface[1] = jnp.concatenate([fs[x + 1, 8:9, :] for x in range(32)], axis=0).astype(BF16)

    pl.semaphore_wait(barrier, len(partners))

    def send(src, dst, s, r, to):
        copy = pltpu.make_async_remote_copy(
            src_ref=src, dst_ref=dst, send_sem=s, recv_sem=r, device_id=to, device_id_type=MESH
        )
        copy.start()
        return copy

    c_ylo = send(yface.at[0], ylo, fsend.at[0], frecv.at[0], at(0, 1))
    c_yhi = send(yface.at[1], yhi, fsend.at[1], frecv.at[1], at(0, -1))
    c_xlo = send(ref_v.at[31], xlo, fsend.at[2], frecv.at[2], at(1, 0))
    c_xhi = send(ref_v.at[0], xhi, fsend.at[3], frecv.at[3], at(-1, 0))
    load_own.wait()
    c_dlo = send(own_v, lo_v, fsend.at[4], frecv.at[4], at(0, 1))
    c_dhi = send(own_v, hi_v, fsend.at[5], frecv.at[5], at(0, -1))
    c_xlo.wait_recv()
    c_xhi.wait_recv()
    c_ylo.wait_recv()
    c_yhi.wait_recv()
    fs[0, 8:40, :] = xlo[...].astype(F32) * xlo_ok
    fs[33, 8:40, :] = xhi[...].astype(F32) * xhi_ok
    face_lo = ylo[...].astype(F32) * ylo_ok
    face_hi = yhi[...].astype(F32) * yhi_ok
    for x in range(32):
        fs[x + 1, 7:8, :] = face_lo[x : x + 1]
        fs[x + 1, 40:41, :] = face_hi[x : x + 1]

    for ey in range(2):
        r = 8 + 16 * ey
        y = slice(16 * ey, 16 * ey + 16)
        moments = []
        for ex in range(2):
            def step(t, carry, ex=ex, r=r, y=y):
                x = 16 * ex + t
                g = (
                    fs[x + 2, r : r + 16, :] - fs[x, r : r + 16, :],
                    fs[x + 1, r + 1 : r + 17, :] - fs[x + 1, r - 1 : r + 15, :],
                    gs[2, x, y, :],
                )
                gs[0, x, y, :] = g[0]
                gs[1, x, y, :] = g[1]
                out = []
                for p, (c, d) in enumerate(PAIRS):
                    s1, s2, s3 = carry[p]
                    s1 = s1 + g[c] * g[d]
                    s2 = s2 + s1
                    s3 = s3 + s2
                    out.append((s1, s2, s3))
                return tuple(out)

            zero = jnp.zeros((16, 128), F32)
            sums = lax.fori_loop(0, 16, step, tuple((zero,) * 3 for _ in PAIRS), unroll=4)
            weighted = []
            for s1, s2, s3 in sums:
                m00 = (2.0 * s3 - s2) * (1.0 / 256.0)
                first = s2 * (1.0 / 16.0)
                weighted.append((m00, first - m00, s1 - 2.0 * first + m00))
            moments.append(weighted)
        for p in range(6):
            (a00, a01, a11), (b00, b01, b11) = moments[0][p], moments[1][p]
            rows = slice(p * 32 + 16 * ey, p * 32 + 16 * ey + 16)
            for u, value in enumerate((a00, a01, a11 + b00, b01, b11)):
                xs[u, rows, :] = value

    t2[40:48, :] = jnp.zeros((8, 640), F32)
    for u in range(5):
        hi, mid, low = pieces(xs[u])
        t = mm(ymat[...], hi) + mm(ymat[...], mid) + mm(ymat[...], low)
        for m in range(5):
            t2[8 * u : 8 * u + 8, 128 * m : 128 * m + 128] = t[8 * m : 8 * m + 8]
    load_w.wait()
    stacked = jnp.concatenate(pieces(t2[...]), axis=0)
    done = mm(stacked, wmat[...])
    done = done[:48] + done[48:96] + done[96:144]
    for u in range(5):
        for group in range(4):
            ksend[group, u] = done[8 * u : 8 * u + 8, 128 * group : 128 * group + 128]

    GROUP = {1: (0, 1), 0: (1, 2), -1: (3, 1)}
    UNIT = {1: (1, 4), 0: (0, 5), -1: (0, 2)}
    kcopies = []
    for n, (dx, dy) in enumerate(NEIGHBOURS):
        g0, gn = GROUP[dy]
        u0, un = UNIT[dx]
        kcopies.append(
            send(
                ksend.at[pl.ds(g0, gn), pl.ds(u0, un)],
                krecv.at[1 - dx, pl.ds(g0, gn), pl.ds(u0, un)],
                ksem_s.at[n], ksem_r.at[n], at(dx, dy),
            )
        )
    krecv[1, 1:3] = ksend[1:3]

    c_dlo.wait_recv()
    c_dhi.wait_recv()
    for ey in range(2):
        r = 8 + 16 * ey
        y = slice(16 * ey, 16 * ey + 16)
        parts = []
        for ex in range(2):
            carry = tuple((jnp.zeros((16, 128), F32),) * 2 for _ in range(3))
            for xb in range(2):
                k = (2 * ex + xb) * 4 + 2 * ey
                off = jnp.concatenate(
                    [jnp.broadcast_to(mask_s[k + h : k + h + 1, :], (8, 128)) for h in range(2)], axis=0
                )
                below, above = off < -0.5, off > 0.5

                def step(t, carry, below=below, above=above, ex=ex, xb=xb, r=r, y=y):
                    x = 16 * ex + 8 * xb + t
                    warped = jnp.where(
                        below, lo_v[x, y, :].astype(F32),
                        jnp.where(above, hi_v[x, y, :].astype(F32), own_v[x, y, :].astype(F32)),
                    )
                    misfit = fs[x + 1, r : r + 16, :] - warped
                    out = []
                    for c in range(3):
                        s1, s2 = carry[c]
                        s1 = s1 + gs[c, x, y, :] * misfit
                        out.append((s1, s2 + s1))
                    return tuple(out)

                carry = lax.fori_loop(0, 8, step, carry, unroll=4)
            parts.append([(s2 * (1.0 / 16.0), s1 - s2 * (1.0 / 16.0)) for s1, s2 in carry])
        for c in range(3):
            (a0, a1_), (b0, b1_) = parts[0][c], parts[1][c]
            rows = slice(c * 32 + 16 * ey, c * 32 + 16 * ey + 16)
            for n, value in enumerate((a0, a1_ + b0, b1_)):
                rx[n, rows, :] = value
    rt2[24:32, :] = jnp.zeros((8, 384), F32)
    for n in range(3):
        hi, mid, low = pieces(rx[n])
        t = mm(yr[...], hi) + mm(yr[...], mid) + mm(yr[...], low)
        for m in range(3):
            rt2[8 * n : 8 * n + 8, 128 * m : 128 * m + 128] = t[8 * m : 8 * m + 8]
    stacked = jnp.concatenate(pieces(rt2[...]), axis=0)
    done = mm(stacked, wr[...])
    done = done[:32] + done[32:64] + done[64:96]
    for n in range(3):
        rsend[n] = done[8 * n : 8 * n + 8]
    rcopies = []
    for n, (bx, by) in enumerate(SOURCES):
        rcopies.append(
            send(rsend, rrecv.at[bx + 2, by + 2], rsem_s.at[n], rsem_r.at[n], at(-bx, -by))
        )
    rrecv[2, 2] = rsend[...]

    lane = lax.broadcasted_iota(jnp.int32, (8, 128), 1)
    sub = lax.broadcasted_iota(jnp.int32, (8, 128), 0)
    slot, depth = lane // 16, lane % 16

    def roll(x, shift):
        shift = shift % 128
        return x if shift == 0 else pltpu.roll(x, shift, 1)

    for copy in kcopies:
        copy.wait_recv()
    in_a_diag = jnp.where(slot == 1, 1.0, jnp.where(slot == 2, ylo_ok, 0.0))
    in_b_diag = (slot >= 2) & (slot <= 4)
    for e in range(9):
        def entry(group, e=e):
            if e == 3:
                return krecv[0, group, 4] * xlo_ok + krecv[1, group, 0]
            if e == 7:
                return krecv[1, group, 4] + krecv[2, group, 0]
            if e < 3:
                return krecv[0, group, e + 1]
            if e < 7:
                return krecv[1, group, e - 3]
            return krecv[2, group, 1]

        a, b0, b1_, c = [entry(group) for group in range(4)]

        def diag(a, b, c):
            return a * in_a_diag + jnp.where(in_b_diag, b, 0.0) + jnp.where(slot == 4, c, 0.0)

        def off_diag(a, b, c):
            return jnp.where(slot < 2, a, jnp.where(slot < 4, b, jnp.where(slot == 4, c, 0.0)))

        dd = diag(roll(a, -16), b0, c)
        fd = off_diag(a, roll(b0, -48), roll(c, -16))
        df = diag(roll(a, -80), b1_, roll(c, -32))
        ff = off_diag(roll(a, -64), roll(b1_, -48), roll(c, -48))
        kf[e, 4] = dd
        kf[e, 5] = df
        kf[e, 3] = roll(df, 1)
        kf[e, 7] = fd
        kf[e, 1] = roll(fd, 16)
        kf[e, 8] = ff
        kf[e, 6] = roll(ff, 1)
        kf[e, 2] = roll(ff, 16)
        kf[e, 0] = roll(ff, 17)

    lane_j = 2 * gy + slot - 2
    lane_ok = (lane_j >= 0) & (lane_j < 64) & (slot < 6) & (depth < 9)
    lane_mask = jnp.where(lane_ok, 1.0, 0.0)
    node_mask = {i: lane_mask * flag((2 * gx + i >= 0) & (2 * gx + i < 16)) for i in range(-2, 4)}
    own_mask = jnp.where((slot >= 2) & (slot < 4) & (depth < 9), 1.0, 0.0)

    def apply(v, rows):
        need = sorted({i + ox for i in rows for ox in (-1, 0, 1)})
        first, second = {}, {}
        for i in need:
            second[i] = v[i]
            first[i] = jnp.where(sub < 3, v[i], pltpu.roll(v[i], 7, 0))
        acc1 = {i: jnp.zeros((8, 128), F32) for i in rows}
        acc2 = {i: jnp.zeros((8, 128), F32) for i in rows}
        for o in range(9):
            oy, oz = o // 3 - 1, o % 3 - 1
            s1 = {i: roll(first[i], -(16 * oy + oz)) for i in need}
            s2 = {i: roll(second[i], -(16 * oy + oz)) for i in need}
            for i in rows:
                for ox in (-1, 0, 1):
                    k = kf[2 * i + 3 + ox, o]
                    acc1[i] = acc1[i] + k * s1[i + ox]
                    acc2[i] = acc2[i] + k * s2[i + ox]
        out = {}
        for i in rows:
            total = acc1[i] + pltpu.roll(acc1[i], 5, 0)
            total = total + jnp.where(sub == 0, pltpu.roll(acc2[i], 3, 0), pltpu.roll(acc2[i], 6, 0))
            out[i] = jnp.where(sub < 3, total, jnp.where(sub < 6, pltpu.roll(total, 3, 0), pltpu.roll(total, 6, 0)))
        return out

    for copy in rcopies:
        copy.wait_recv()
    w0 = {}
    lo2_x, lo2_y = flag(gx > 1), flag(gy > 1)
    x_ok = {-2: lo2_x, -1: xlo_ok, 0: None, 1: None}
    y_ok = {-2: lo2_y, -1: ylo_ok, 0: None, 1: None}
    for i in range(-2, 4):
        total = None
        for by in (-2, -1, 0, 1):
            part = None
            for bx in (-2, -1, 0, 1):
                n = i - 2 * bx
                if 0 <= n <= 2:
                    term = rrecv[bx + 2, by + 2, n]
                    if x_ok[bx] is not None:
                        term = term * x_ok[bx]
                    part = term if part is None else part + term
            part = roll(part, 32 * by)
            if y_ok[by] is not None:
                part = part * y_ok[by]
            total = part if total is None else total + part
        w0[i] = total * node_mask[i]

    w1 = apply(w0, (-1, 0, 1, 2))
    w1 = {i: w1[i] * node_mask[i] for i in w1}
    w2_own = apply(w1, (0, 1))
    for i in range(2):
        vsend[i] = w2_own[i] * own_mask
    vcopies = []
    for n, (dx, dy) in enumerate(NEIGHBOURS):
        vcopies.append(
            send(vsend, vrecv.at[1 - dx, 1 - dy], vsem_s.at[n], vsem_r.at[n], at(dx, dy))
        )
    vrecv[1, 1] = vsend[...]

    counted = jnp.where(sub < 3, own_mask, 0.0)

    def dots(rows_of_pairs, count):
        out = []
        for a, b in rows_of_pairs:
            product = (a[0] * b[0] + a[1] * b[1]) * counted
            out.append(jnp.sum(product, axis=0, keepdims=True))
        out += [jnp.zeros((1, 128), F32)] * (count - len(out))
        return jnp.concatenate(out, axis=0)

    def all_sum(value, which, src_a, slots_a, src_b, slots_b):
        src_a[...] = value
        slots_a[gy] = value
        copies = []
        for m in range(1, NGY):
            copies.append(send(src_a, slots_a.at[gy], arsem_s.at[which, 0], arsem_r.at[which, 0], at(0, m)))
        def finish():
            pltpu.make_async_copy(slots_a.at[pl.ds(0, NGY - 1)], slots_a.at[pl.ds(0, NGY - 1)], arsem_r.at[which, 0]).wait()
            part = jnp.sum(slots_a[...], axis=0)
            src_b[...] = part
            slots_b[gx] = part
            for m in range(1, NGX):
                send(src_b, slots_b.at[gx], arsem_s.at[which, 1], arsem_r.at[which, 1], at(m, 0))
            pltpu.make_async_copy(slots_b.at[pl.ds(0, NGX - 1)], slots_b.at[pl.ds(0, NGX - 1)], arsem_r.at[which, 1]).wait()
            return jnp.sum(jnp.sum(slots_b[...], axis=0), axis=1, keepdims=True)
        return finish

    finish = all_sum(dots([(w0, w0), (w0, w1), (w1, w1)], 8), 0, asrc, a1, b1src, b1)

    for copy in vcopies:
        copy.wait_recv()
    w2 = {}
    for i in range(-2, 4):
        bx, n = i // 2, i % 2
        total = vrecv[bx + 1, 1, n] + roll(vrecv[bx + 1, 0, n], -32) + roll(vrecv[bx + 1, 2, n], 32)
        w2[i] = total * node_mask[i]
    w3 = apply(w2, (-1, 0, 1, 2))
    w3 = {i: w3[i] * node_mask[i] for i in w3}

    sums = finish()
    m0, m1, m2 = sums[0:1], sums[1:2], sums[2:3]
    mu = m1 / m0
    var = jnp.maximum(m2 / m0 - mu * mu, 1e-6 * mu * mu)
    sigma = jnp.sqrt(var)
    inv = 1.0 / sigma
    rows = (-1, 0, 1, 2)
    q0 = {i: w0[i] for i in rows}
    q1 = {i: (w1[i] - mu * w0[i]) * inv for i in rows}
    kq1 = {i: (w2[i] - mu * w1[i]) * inv for i in rows}
    kkq1 = {i: (w3[i] - mu * w2[i]) * inv for i in rows}
    q2 = {i: (kq1[i] - mu * q1[i]) * inv - q0[i] for i in rows}
    kq2 = {i: (kkq1[i] - mu * kq1[i]) * inv - w1[i] for i in rows}
    q3 = {i: (kq2[i] - mu * q2[i]) * inv - q1[i] for i in rows}
    kq3 = apply(q3, (0, 1))
    q4 = {i: (kq3[i] - mu * q3[i]) * inv - q2[i] for i in (0, 1)}
    basis = [q0, q1, q2, q3, q4]
    pairs = [(i, j) for i in range(5) for j in range(i, 5) if (i, j) != (4, 4)]
    gram = all_sum(dots([(basis[i], basis[j]) for i, j in pairs], 16), 1, asrc2, a2, b2src, b2)()
    G = {}
    for n, (i, j) in enumerate(pairs):
        G[i, j] = G[j, i] = gram[n : n + 1]

    def form(left, right):
        total = None
        for i, a in enumerate(left):
            if a is None:
                continue
            inner = None
            for j, b in enumerate(right):
                if b is None:
                    continue
                term = G[i, j] * b
                inner = term if inner is None else inner + term
            term = a * inner
            total = term if total is None else total + term
        return total

    def add(a, b):
        return b if a is None else (a if b is None else a + b)

    one = jnp.ones_like(m0)
    center = mu + DAMPING
    residual = [one, None, None, None, None]
    direction = list(residual)
    update = [None] * 5
    rr = G[0, 0]
    for turn in range(ITERS):
        image = [None] * 5
        for k in range(4):
            d = direction[k]
            if d is None:
                continue
            image[k] = add(image[k], center * d)
            image[k + 1] = add(image[k + 1], sigma * d)
            if k:
                image[k - 1] = add(image[k - 1], sigma * d)
        alpha = rr / form(direction, image)
        update = [add(u, None if d is None else alpha * d) for u, d in zip(update, direction)]
        residual = [add(r, None if q is None else -(alpha * q)) for r, q in zip(residual, image)]
        if turn < ITERS - 1:
            new = form(residual, residual)
            beta = new / rr
            direction = [add(r, None if d is None else beta * d) for r, d in zip(residual, direction)]
            rr = new
    for coords, out in ((update, upd_out), (residual, res_out)):
        for i in range(2):
            total = None
            for k in range(5):
                if coords[k] is not None:
                    term = coords[k] * basis[k][i]
                    total = term if total is None else total + term
            for j in range(2):
                moved = roll(total, -(32 + 16 * j))
                for c in range(3):
                    out[c, i, j : j + 1, :] = moved[c : c + 1, :9]

    for copy in (c_ylo, c_yhi, c_xlo, c_xhi, c_dlo, c_dhi, *kcopies, *rcopies, *vcopies):
        copy.wait_send()
    for which, (slots_a, slots_b) in enumerate(((a1, b1), (a2, b2))):
        pltpu.make_async_copy(slots_a.at[pl.ds(0, NGY - 1)], slots_a.at[pl.ds(0, NGY - 1)], arsem_s.at[which, 0]).wait()
        pltpu.make_async_copy(slots_b.at[pl.ds(0, NGX - 1)], slots_b.at[pl.ds(0, NGX - 1)], arsem_s.at[which, 1]).wait()


def local(reference_scan, deformed_scan, source_column):
    table = source_column.reshape(NGY, 1, 64)
    consts = constants()
    vmem = pl.BlockSpec(memory_space=pltpu.VMEM)
    hbm = pl.BlockSpec(memory_space=pl.ANY)
    V, DMA = pltpu.VMEM, pltpu.SemaphoreType.DMA
    scratch = [
        V((32, 32, 128), BF16), V((32, 32, 128), BF16), V((32, 32, 128), BF16), V((32, 32, 128), BF16),
        V((34, 48, 128), F32), V((3, 32, 32, 128), F32), V((16, 128), F32),
        V((2, 32, 128), BF16), V((32, 128), BF16), V((32, 128), BF16), V((32, 128), BF16), V((32, 128), BF16),
        V((5, 192, 128), F32), V((48, 640), F32), V((4, 5, 8, 128), F32), V((3, 4, 5, 8, 128), F32),
        V((3, 96, 128), F32), V((32, 384), F32), V((3, 8, 128), F32), V((4, 4, 3, 8, 128), F32),
        V((9, 9, 8, 128), F32), V((640, 512), BF16), V((2, 8, 128), F32), V((3, 3, 2, 8, 128), F32),
        V((8, 128), F32), V((NGY, 8, 128), F32), V((8, 128), F32), V((NGX, 8, 128), F32),
        V((16, 128), F32), V((NGY, 16, 128), F32), V((16, 128), F32), V((NGX, 16, 128), F32),
        DMA((3,)), DMA((6,)), DMA((6,)), DMA((8,)), DMA((8,)), DMA((15,)), DMA((15,)), DMA((8,)), DMA((8,)),
        DMA((2, 2)), DMA((2, 2)),
    ]
    out = jax.ShapeDtypeStruct((3, 2, 2, 9), F32)
    return pl.pallas_call(
        kernel,
        out_shape=(out, out),
        in_specs=[hbm, hbm, vmem, vmem, hbm, vmem, vmem, vmem, vmem],
        out_specs=(vmem, vmem),
        scratch_shapes=scratch,
        compiler_params=pltpu.CompilerParams(
            collective_id=0, has_side_effects=True, vmem_limit_bytes=40 * 1024 * 1024
        ),
    )(reference_scan, deformed_scan, table, *consts)


def solution(mesh):
    return jax.shard_map(
        local,
        mesh=mesh,
        in_specs=(P("gx", "gy", None), P("gx", "gy", None), P("gx", None, None, None)),
        out_specs=(P(None, "gx", "gy", None), P(None, "gx", "gy", None)),
        check_vma=False,
    )
```

time: 692 us -> 55.8 us (0.08)
  blocking collectives: 549 us -> 0 us
  starting transfers between devices: 64.4 us -> 0 us
  Pallas kernels: 0 us -> 46 us
  waiting for transfers between devices: 31.2 us -> 0 us
  matrix products: 18.5 us -> 0 us
  other arithmetic: 12.3 us -> 0 us
  between operations: 10.8 us -> 0.66 us
    psum x7 -> x0, blocking collectives: 549 us -> none  [the longest x4 311 us: squares(): return lax.psum(inner(residual, residual), ('gx', 'gy'))]
    ppermute x24 -> x0, starting transfers between devices: 64.4 us -> none  [the longest x18 46 us: passed_along(): lax.ppermute(value, axis, [(source, source + steps) for source in range(l...]
    pallas_call x0 -> x1, Pallas kernels: none -> 46 us  [local(): pl.pallas_call(kernel, out_shape=(out, out), in_specs=[hbm, hbm, vmem, vm...]
    ppermute x24 -> x0, waiting for transfers between devices: 31.2 us -> none  [the longest x18 30.4 us: passed_along(): lax.ppermute(value, axis, [(source, source + steps) for source in range(l...]
    dot_general x27 -> x0, matrix products: 18.5 us -> none  [the longest x5 8.5 us: fold_back(): temp = jnp.einsum('cxyz,xi->ciyz', voxels, matrix_x, precision=highest)]
    reduce_sum x11 -> x0, other arithmetic: 8.92 us -> none  [the longest x4 4.64 us: local(): along = jnp.sum(gradient * moved, axis=0)]
    unnamed x13 -> x20, local copies, waits for them, and re-layouts: 1.03 us -> 8.69 us
  transfers between devices with their start and end apart: 24 -> 0, of which waited for: 19 -> 0; matrix products, arithmetic and copies ran while one was open for 1% -> 0% of each run, Pallas kernels for 0% -> 0%
where the time goes in v1:
time: 55.8 us; the launch traced here: 55.3 us
  Pallas kernels  46 us (82%)
  local copies, waits for them, and re-layouts  8.69 us (16%)
  between operations  0.66 us (1%)
    pallas_call x1, Pallas kernels, local(): pl.pallas_call(kernel, out_shape=(out, out), in_specs=[hbm, hbm, vmem, vm...  46 us
    unnamed x20, local copies, waits for them, and re-layouts  8.69 us

profile of v1, /device:TPU:1, one launch (start us, length us, event | category | flops | bytes accessed | tf_op | source)
XLA Modules:
  0.0 55.3 jit_solution(17662952618409848386)
XLA Ops:
  0.6 0.0 copy-start
  0.6 1.1 %copy-done = bf16[640,512]{1,0:T(8,128)(2,1)S(1)} copy-done((bf16[640,512]{1,0:T(8,128)(2,1)S(1)}, bf16[640,512]{1,0:T(8,128)(2,1)}, u32[]{:S(2)}) %copy-start) | copy-done | bytes 655384
  1.7 0.0 copy-start.1
  1.7 0.9 %copy-done.1 = bf16[32,32,128]{2,1,0:T(8,128)(2,1)S(1)} copy-done((bf16[32,32,128]{2,1,0:T(8,128)(2,1)S(1)}, bf16[32,32,128]{2,1,0:T(8,128)(2,1)}, u32[]{:S(2)}) %copy-start.1) | copy-done | bytes 262168
  2.7 0.0 copy-start.2
  2.7 0.9 %copy-done.2 = bf16[32,32,128]{2,1,0:T(8,128)(2,1)S(1)} copy-done((bf16[32,32,128]{2,1,0:T(8,128)(2,1)S(1)}, bf16[32,32,128]{2,1,0:T(8,128)(2,1)}, u32[]{:S(2)}) %copy-start.2) | copy-done | bytes 262168
  3.6 0.0 copy-start.3
  3.6 0.9 %copy-done.3 = bf16[384,128]{1,0:T(8,128)(2,1)S(1)} copy-done((bf16[384,128]{1,0:T(8,128)(2,1)S(1)}, bf16[384,128]{1,0:T(8,128)(2,1)}, u32[]{:S(2)}) %copy-start.3) | copy-done | bytes 98328
  4.5 0.0 copy-start.4
  4.5 0.8 %copy-done.4 = bf16[128,128]{1,0:T(8,128)(2,1)S(1)} copy-done((bf16[128,128]{1,0:T(8,128)(2,1)S(1)}, bf16[128,128]{1,0:T(8,128)(2,1)}, u32[]{:S(2)}) %copy-start.4) | copy-done | bytes 32792
  5.3 0.0 copy-start.5
  5.3 0.7 %copy-done.5 = bf16[48,192]{1,0:T(8,128)(2,1)S(1)} copy-done((bf16[48,192]{1,0:T(8,128)(2,1)S(1)}, bf16[48,192]{1,0:T(8,128)(2,1)}, u32[]{:S(2)}) %copy-start.5) | copy-done | bytes 18456
  6.0 0.0 copy-start.6
  6.0 0.7 %copy-done.6 = s32[1,32,64,1]{2,3,1,0:T(1,128)S(1)} copy-done((s32[1,32,64,1]{2,3,1,0:T(1,128)S(1)}, s32[1,32,64,1]{2,3,1,0:T(1,128)}, u32[]{:S(2)}) %copy-start.6) | copy-done | bytes 8216
  6.7 0.0 copy-start.7
  6.7 0.7 %copy-done.7 = bf16[64,128]{1,0:T(8,128)(2,1)S(1)} copy-done((bf16[64,128]{1,0:T(8,128)(2,1)S(1)}, bf16[64,128]{1,0:T(8,128)(2,1)}, u32[]{:S(2)}) %copy-start.7) | copy-done | bytes 16408
  7.4 0.0 copy-start.8
  7.4 0.7 %copy-done.8 = bf16[32,96]{1,0:T(8,128)(2,1)S(1)} copy-done((bf16[32,96]{1,0:T(8,128)(2,1)S(1)}, bf16[32,96]{1,0:T(8,128)(2,1)}, u32[]{:S(2)}) %copy-start.8) | copy-done | bytes 6168
  8.1 46.0 %shard_map.104 = (f32[3,2,2,9]{3,2,1,0:T(2,128)S(1)}, f32[3,2,2,9]{3,2,1,0:T(2,128)S(1)}) custom-call(bf16[32,32,128]{2,1,0:T(8,128)(2,1)S(1)} %copy-done.1, bf16[32,32,128]{2,1,0:T(8,128)(2,1)S(1)} %copy-done.2, s32[32,1,64]{2,1,0:T(1,128)S(1)} %bitcast.1, bf16[48,192]{1,0:T(8,128)(2,1)S(1)} %copy-done.5, bf16[640,512]{1,0:T(8,128)(2,1)S(1)} %copy-done, ...), custom_call_target="tpu_custom_call" | custom-call | tf_op jit(solution)/shard_map/pallas_call | solution.py:543
  54.1 0.6 %copy.13 = f32[3,2,2,9]{3,2,1,0:T(2,128)} copy(f32[3,2,2,9]{3,2,1,0:T(2,128)S(1)} %get-tuple-element.4) | data formatting | bytes 864
  54.7 0.6 %copy.14 = f32[3,2,2,9]{3,2,1,0:T(2,128)} copy(f32[3,2,2,9]{3,2,1,0:T(2,128)S(1)} %get-tuple-element.5) | data formatting | bytes 864
Async XLA Ops:
  0.6 1.1 %copy-start = (bf16[640,512]{1,0:T(8,128)(2,1)S(1)}, bf16[640,512]{1,0:T(8,128)(2,1)}, u32[]{:S(2)}) copy-start(bf16[640,512]{1,0:T(8,128)(2,1)} %constant.13.clone.wmat_h) | copy-start | bytes 1966084
  1.7 0.9 %copy-start.1 = (bf16[32,32,128]{2,1,0:T(8,128)(2,1)S(1)}, bf16[32,32,128]{2,1,0:T(8,128)(2,1)}, u32[]{:S(2)}) copy-start(bf16[32,32,128]{2,1,0:T(8,128)(2,1)} %ref_h.1) | copy-start | bytes 786436
  2.7 0.9 %copy-start.2 = (bf16[32,32,128]{2,1,0:T(8,128)(2,1)S(1)}, bf16[32,32,128]{2,1,0:T(8,128)(2,1)}, u32[]{:S(2)}) copy-start(bf16[32,32,128]{2,1,0:T(8,128)(2,1)} %def_h.1) | copy-start | bytes 786436
  3.6 0.9 %copy-start.3 = (bf16[384,128]{1,0:T(8,128)(2,1)S(1)}, bf16[384,128]{1,0:T(8,128)(2,1)}, u32[]{:S(2)}) copy-start(bf16[384,128]{1,0:T(8,128)(2,1)} %constant.15.clone.wr) | copy-start | bytes 294916
  4.5 0.8 %copy-start.4 = (bf16[128,128]{1,0:T(8,128)(2,1)S(1)}, bf16[128,128]{1,0:T(8,128)(2,1)}, u32[]{:S(2)}) copy-start(bf16[128,128]{1,0:T(8,128)(2,1)} %constant.16.clone.dz) | copy-start | bytes 98308
  5.3 0.7 %copy-start.5 = (bf16[48,192]{1,0:T(8,128)(2,1)S(1)}, bf16[48,192]{1,0:T(8,128)(2,1)}, u32[]{:S(2)}) copy-start(bf16[48,192]{1,0:T(8,128)(2,1)} %constant.12.clone.ymat) | copy-start | bytes 55300
  6.0 0.7 %copy-start.6 = (s32[1,32,64,1]{2,3,1,0:T(1,128)S(1)}, s32[1,32,64,1]{2,3,1,0:T(1,128)}, u32[]{:S(2)}) copy-start(s32[1,32,64,1]{2,3,1,0:T(1,128)} %param.11) | copy-start | bytes 24580
  6.7 0.7 %copy-start.7 = (bf16[64,128]{1,0:T(8,128)(2,1)S(1)}, bf16[64,128]{1,0:T(8,128)(2,1)}, u32[]{:S(2)}) copy-start(bf16[64,128]{1,0:T(8,128)(2,1)} %constant.17.clone.spread) | copy-start | bytes 49156
  7.4 0.7 %copy-start.8 = (bf16[32,96]{1,0:T(8,128)(2,1)S(1)}, bf16[32,96]{1,0:T(8,128)(2,1)}, u32[]{:S(2)}) copy-start(bf16[32,96]{1,0:T(8,128)(2,1)} %constant.14.clone.yr) | copy-start | bytes 18436

commit v2 on v1

--- a/solution.py
+++ b/solution.py
@@ -76,7 +76,6 @@
             dz[z - 1, z] = -1.0
     lanes = np.arange(128)
     spread = (np.arange(64)[:, None] % 4 == lanes[None, :] // 32).astype(np.float64)
-    small = np.zeros((256, 256))
     cast = lambda a: a.astype(ml_dtypes.bfloat16)
     return [cast(a) for a in (ymat, wmat, yr, wr, dz, spread)]
 
@@ -89,16 +88,39 @@
     return hi, mid, low
 
 
+def two_sum(a, b):
+    s = a + b
+    t = s - a
+    return s, (a - (s - t)) + (b - t)
+
+
+def split(a):
+    t = a * 4097.0
+    high = t - (t - a)
+    return high, a - high
+
+
+def two_prod(a, a_halves, b, b_halves):
+    p = a * b
+    (ah, al), (bh, bl) = a_halves, b_halves
+    return p, ((ah * bh - p) + ah * bl + al * bh) + al * bl
+
+
+def add(a, b):
+    return b if a is None else (a if b is None else a + b)
+
+
 def mm(a, b):
     return jnp.dot(a, b, preferred_element_type=F32)
 
 
 def kernel(
-    ref_h, def_h, table, ymat, wmat_h, yr, wr, dz, spread,
+    ref_h, def_h, table_h, ymat_h, wmat_h, yr_h, wr_h, dz_h, spread_h,
     upd_out, res_out,
+    table, ymat, yr, wr, dz, spread,
     ref_v, own_v, lo_v, hi_v, fs, gs, mask_s, yface, xlo, xhi, ylo, yhi,
     xs, t2, ksend, krecv, rx, rt2, rsend, rrecv, kf, wmat, vsend, vrecv,
-    asrc, a1, b1src, b1, asrc2, a2, b2src, b2,
+    asrc, a1, b1src, b1,
     lsem, fsend, frecv, ksem_s, ksem_r, rsem_s, rsem_r, vsem_s, vsem_r, arsem_s, arsem_r,
 ):
     gx, gy = lax.axis_index("gx"), lax.axis_index("gy")
@@ -115,9 +137,10 @@
     load_ref = pltpu.make_async_copy(ref_h, ref_v, lsem.at[0])
     load_own = pltpu.make_async_copy(def_h, own_v, lsem.at[1])
     load_w = pltpu.make_async_copy(wmat_h, wmat, lsem.at[2])
-    load_ref.start()
-    load_own.start()
-    load_w.start()
+    small = [(table_h.at[gy], table), (spread_h, spread), (dz_h, dz), (ymat_h, ymat), (yr_h, yr), (wr_h, wr)]
+    small = [pltpu.make_async_copy(src, dst, lsem.at[3 + n]) for n, (src, dst) in enumerate(small)]
+    for copy in (load_ref, *small, load_own, load_w):
+        copy.start()
 
     def flag(condition):
         return jnp.where(condition, 1.0, 0.0).astype(F32)
@@ -125,7 +148,9 @@
     xlo_ok, xhi_ok = flag(gx > 0), flag(gx < NGX - 1)
     ylo_ok, yhi_ok = flag(gy > 0), flag(gy < NGY - 1)
 
-    row = (table[gy] - gy).astype(F32)
+    for copy in small:
+        copy.wait()
+    row = (table[...] - gy).astype(F32)
     r16 = lax.broadcasted_iota(jnp.int32, (16, 64), 0)
     c64 = lax.broadcasted_iota(jnp.int32, (16, 64), 1)
     picked = jnp.where(c64 // 4 == r16, jnp.broadcast_to(row, (16, 64)), 0.0).astype(BF16)
@@ -398,35 +423,6 @@
         )
     vrecv[1, 1] = vsend[...]
 
-    counted = jnp.where(sub < 3, own_mask, 0.0)
-
-    def dots(rows_of_pairs, count):
-        out = []
-        for a, b in rows_of_pairs:
-            product = (a[0] * b[0] + a[1] * b[1]) * counted
-            out.append(jnp.sum(product, axis=0, keepdims=True))
-        out += [jnp.zeros((1, 128), F32)] * (count - len(out))
-        return jnp.concatenate(out, axis=0)
-
-    def all_sum(value, which, src_a, slots_a, src_b, slots_b):
-        src_a[...] = value
-        slots_a[gy] = value
-        copies = []
-        for m in range(1, NGY):
-            copies.append(send(src_a, slots_a.at[gy], arsem_s.at[which, 0], arsem_r.at[which, 0], at(0, m)))
-        def finish():
-            pltpu.make_async_copy(slots_a.at[pl.ds(0, NGY - 1)], slots_a.at[pl.ds(0, NGY - 1)], arsem_r.at[which, 0]).wait()
-            part = jnp.sum(slots_a[...], axis=0)
-            src_b[...] = part
-            slots_b[gx] = part
-            for m in range(1, NGX):
-                send(src_b, slots_b.at[gx], arsem_s.at[which, 1], arsem_r.at[which, 1], at(m, 0))
-            pltpu.make_async_copy(slots_b.at[pl.ds(0, NGX - 1)], slots_b.at[pl.ds(0, NGX - 1)], arsem_r.at[which, 1]).wait()
-            return jnp.sum(jnp.sum(slots_b[...], axis=0), axis=1, keepdims=True)
-        return finish
-
-    finish = all_sum(dots([(w0, w0), (w0, w1), (w1, w1)], 8), 0, asrc, a1, b1src, b1)
-
     for copy in vcopies:
         copy.wait_recv()
     w2 = {}
@@ -436,29 +432,112 @@
         w2[i] = total * node_mask[i]
     w3 = apply(w2, (-1, 0, 1, 2))
     w3 = {i: w3[i] * node_mask[i] for i in w3}
-
-    sums = finish()
-    m0, m1, m2 = sums[0:1], sums[1:2], sums[2:3]
-    mu = m1 / m0
-    var = jnp.maximum(m2 / m0 - mu * mu, 1e-6 * mu * mu)
-    sigma = jnp.sqrt(var)
-    inv = 1.0 / sigma
-    rows = (-1, 0, 1, 2)
-    q0 = {i: w0[i] for i in rows}
-    q1 = {i: (w1[i] - mu * w0[i]) * inv for i in rows}
-    kq1 = {i: (w2[i] - mu * w1[i]) * inv for i in rows}
-    kkq1 = {i: (w3[i] - mu * w2[i]) * inv for i in rows}
-    q2 = {i: (kq1[i] - mu * q1[i]) * inv - q0[i] for i in rows}
-    kq2 = {i: (kkq1[i] - mu * kq1[i]) * inv - w1[i] for i in rows}
-    q3 = {i: (kq2[i] - mu * q2[i]) * inv - q1[i] for i in rows}
-    kq3 = apply(q3, (0, 1))
-    q4 = {i: (kq3[i] - mu * q3[i]) * inv - q2[i] for i in (0, 1)}
-    basis = [q0, q1, q2, q3, q4]
-    pairs = [(i, j) for i in range(5) for j in range(i, 5) if (i, j) != (4, 4)]
-    gram = all_sum(dots([(basis[i], basis[j]) for i, j in pairs], 16), 1, asrc2, a2, b2src, b2)()
+    w4 = apply(w3, (0, 1))
+    krylov = [w0, w1, w2, w3, w4]
+
+    packed = [jnp.where(sub < 3, w[0], jnp.where(sub < 6, w[1], 0.0)) * own_mask for w in krylov]
+    left = roll(packed[0], -32) + packed[1] + roll(packed[2], 32) + roll(packed[3], 64)
+    left_halves = split(left)
+    value = remainder = jnp.zeros((8, 128), F32)
+    for j in range(5):
+        right = packed[j] + roll(packed[j], 32)
+        right = right + roll(right, 64)
+        p, e = two_prod(left, left_halves, right, split(right))
+        for shift in (4, 2, 1):
+            p, err = two_sum(p, pltpu.roll(p, shift, 0))
+            e = e + pltpu.roll(e, shift, 0) + err
+        value = jnp.where(sub == j, p, value)
+        remainder = jnp.where(sub == j, e, remainder)
+
+    def pair_tree(slots):
+        p, e = slots[:, 0], slots[:, 1]
+        while p.shape[0] > 1:
+            half = p.shape[0] // 2
+            e = e[:half] + e[half:]
+            p, err = two_sum(p[:half], p[half:])
+            e = e + err
+        return p[0], e[0]
+
+    asrc[0] = value
+    asrc[1] = remainder
+    a1[gy] = asrc[...]
+    for m in range(1, NGY):
+        send(asrc, a1.at[gy], arsem_s.at[0], arsem_r.at[0], at(0, m))
+    pltpu.make_async_copy(a1.at[pl.ds(0, NGY - 1)], a1.at[pl.ds(0, NGY - 1)], arsem_r.at[0]).wait()
+    p, e = pair_tree(a1[...])
+    b1src[0] = p
+    b1src[1] = e
+    b1[gx] = b1src[...]
+    for m in range(1, NGX):
+        send(b1src, b1.at[gx], arsem_s.at[1], arsem_r.at[1], at(m, 0))
+    pltpu.make_async_copy(b1.at[pl.ds(0, NGX - 1)], b1.at[pl.ds(0, NGX - 1)], arsem_r.at[1]).wait()
+    p, e = pair_tree(b1[...])
+    for shift in (16, 8, 4, 2, 1):
+        e = e + roll(e, -shift)
+        p, err = two_sum(p, roll(p, -shift))
+        e = e + err
+    high = p + e
+    low = (p - high) + e
+
+    def few_bits(x):
+        t = x * 262145.0
+        return t - (t - x)
+
+    m0, m1, m2 = high[0:1, 0:1], high[1:2, 0:1], high[1:2, 32:33]
+    mean = m1 / m0
+    mu = few_bits(mean)
+    spread_q = few_bits(jnp.maximum(m2 / m0 - mean * mean, 1e-5 * mean * mean))
+    poly = [[jnp.ones_like(m0)]]
+    for k in range(4):
+        new = [None] + list(poly[k])
+        for i, a in enumerate(poly[k]):
+            new[i] = add(new[i], -(mu * a))
+        if k:
+            for i, a in enumerate(poly[k - 1]):
+                new[i] = new[i] - spread_q * a
+        poly.append(new)
+
+    def combine(coefficients, terms):
+        total = None
+        for c, (h, l) in zip(coefficients, terms):
+            c = jnp.broadcast_to(c, h.shape)
+            p, e = two_prod(c, split(c), h, split(h))
+            e = e + c * l
+            if total is None:
+                total = (p, e)
+            else:
+                q, err = two_sum(total[0], p)
+                total = (q, total[1] + e + err)
+        h = total[0] + total[1]
+        return h, (total[0] - h) + total[1]
+
+    rows_w = [(high[j : j + 1], low[j : j + 1]) for j in range(5)]
+    rows_q = [combine(poly[k], rows_w) for k in range(5)]
+    filler = [jnp.zeros((3, 128), F32)]
+    mixed = [jnp.concatenate([r[n] for r in rows_q] + filler, axis=0) for n in range(2)]
+    moved = [tuple(roll(x, -32 * t) for x in mixed) for t in range(4)]
     G = {}
-    for n, (i, j) in enumerate(pairs):
-        G[i, j] = G[j, i] = gram[n : n + 1]
+    for l in range(4):
+        h, _ = combine(poly[l], moved)
+        for k in range(l, 5):
+            G[k, l] = G[l, k] = h[k : k + 1, 0:1]
+
+    own = (0, 1)
+
+    def times(k_of, v, older):
+        return {i: k_of[i] - mu * v[i] - (0.0 if older is None else spread_q * older[i]) for i in own}
+
+    q1 = times(w1, w0, None)
+    kq1 = times(w2, w1, None)
+    kkq1 = times(w3, w2, None)
+    kkkq1 = times(w4, w3, None)
+    q2 = times(kq1, q1, w0)
+    kq2 = times(kkq1, kq1, w1)
+    kkq2 = times(kkkq1, kkq1, w2)
+    q3 = times(kq2, q2, q1)
+    kq3 = times(kkq2, kq2, kq1)
+    q4 = times(kq3, q3, q2)
+    basis = [w0, q1, q2, q3, q4]
 
     def form(left, right):
         total = None
@@ -475,9 +554,6 @@
             total = term if total is None else total + term
         return total
 
-    def add(a, b):
-        return b if a is None else (a if b is None else a + b)
-
     one = jnp.ones_like(m0)
     center = mu + DAMPING
     residual = [one, None, None, None, None]
@@ -491,9 +567,9 @@
             if d is None:
                 continue
             image[k] = add(image[k], center * d)
-            image[k + 1] = add(image[k + 1], sigma * d)
+            image[k + 1] = add(image[k + 1], d)
             if k:
-                image[k - 1] = add(image[k - 1], sigma * d)
+                image[k - 1] = add(image[k - 1], spread_q * d)
         alpha = rr / form(direction, image)
         update = [add(u, None if d is None else alpha * d) for u, d in zip(update, direction)]
         residual = [add(r, None if q is None else -(alpha * q)) for r, q in zip(residual, image)]
@@ -516,34 +592,33 @@
 
     for copy in (c_ylo, c_yhi, c_xlo, c_xhi, c_dlo, c_dhi, *kcopies, *rcopies, *vcopies):
         copy.wait_send()
-    for which, (slots_a, slots_b) in enumerate(((a1, b1), (a2, b2))):
-        pltpu.make_async_copy(slots_a.at[pl.ds(0, NGY - 1)], slots_a.at[pl.ds(0, NGY - 1)], arsem_s.at[which, 0]).wait()
-        pltpu.make_async_copy(slots_b.at[pl.ds(0, NGX - 1)], slots_b.at[pl.ds(0, NGX - 1)], arsem_s.at[which, 1]).wait()
+    pltpu.make_async_copy(a1.at[pl.ds(0, NGY - 1)], a1.at[pl.ds(0, NGY - 1)], arsem_s.at[0]).wait()
+    pltpu.make_async_copy(b1.at[pl.ds(0, NGX - 1)], b1.at[pl.ds(0, NGX - 1)], arsem_s.at[1]).wait()
 
 
 def local(reference_scan, deformed_scan, source_column):
     table = source_column.reshape(NGY, 1, 64)
     consts = constants()
     vmem = pl.BlockSpec(memory_space=pltpu.VMEM)
-    hbm = pl.BlockSpec(memory_space=pl.ANY)
+    hbm = pl.BlockSpec(memory_space=pltpu.HBM)
     V, DMA = pltpu.VMEM, pltpu.SemaphoreType.DMA
     scratch = [
+        V((1, 64), jnp.int32), V((48, 192), BF16), V((32, 96), BF16), V((384, 128), BF16), V((128, 128), BF16), V((64, 128), BF16),
         V((32, 32, 128), BF16), V((32, 32, 128), BF16), V((32, 32, 128), BF16), V((32, 32, 128), BF16),
         V((34, 48, 128), F32), V((3, 32, 32, 128), F32), V((16, 128), F32),
         V((2, 32, 128), BF16), V((32, 128), BF16), V((32, 128), BF16), V((32, 128), BF16), V((32, 128), BF16),
         V((5, 192, 128), F32), V((48, 640), F32), V((4, 5, 8, 128), F32), V((3, 4, 5, 8, 128), F32),
         V((3, 96, 128), F32), V((32, 384), F32), V((3, 8, 128), F32), V((4, 4, 3, 8, 128), F32),
         V((9, 9, 8, 128), F32), V((640, 512), BF16), V((2, 8, 128), F32), V((3, 3, 2, 8, 128), F32),
-        V((8, 128), F32), V((NGY, 8, 128), F32), V((8, 128), F32), V((NGX, 8, 128), F32),
-        V((16, 128), F32), V((NGY, 16, 128), F32), V((16, 128), F32), V((NGX, 16, 128), F32),
-        DMA((3,)), DMA((6,)), DMA((6,)), DMA((8,)), DMA((8,)), DMA((15,)), DMA((15,)), DMA((8,)), DMA((8,)),
-        DMA((2, 2)), DMA((2, 2)),
+        V((2, 8, 128), F32), V((NGY, 2, 8, 128), F32), V((2, 8, 128), F32), V((NGX, 2, 8, 128), F32),
+        DMA((9,)), DMA((6,)), DMA((6,)), DMA((8,)), DMA((8,)), DMA((15,)), DMA((15,)), DMA((8,)), DMA((8,)),
+        DMA((2,)), DMA((2,)),
     ]
     out = jax.ShapeDtypeStruct((3, 2, 2, 9), F32)
     return pl.pallas_call(
         kernel,
         out_shape=(out, out),
-        in_specs=[hbm, hbm, vmem, vmem, hbm, vmem, vmem, vmem, vmem],
+        in_specs=[hbm] * 9,
         out_specs=(vmem, vmem),
         scratch_shapes=scratch,
         compiler_params=pltpu.CompilerParams(

time: 55.8 us -> 50.4 us (0.903)
  Pallas kernels: 46 us -> 40.6 us
    pallas_call x1, Pallas kernels: 46 us -> 40.6 us  [local(): pl.pallas_call(kernel, out_shape=(out, out), in_specs=[hbm] * 9, out_spec...]
where the time goes in v2:
time: 50.4 us; the launch traced here: 49.9 us
  Pallas kernels  40.6 us (81%)
  local copies, waits for them, and re-layouts  8.69 us (17%)
  between operations  0.66 us (1%)
    pallas_call x1, Pallas kernels, local(): pl.pallas_call(kernel, out_shape=(out, out), in_specs=[hbm] * 9, out_spec...  40.6 us
    unnamed x20, local copies, waits for them, and re-layouts  8.69 us

profile of v2, /device:TPU:1, one launch (start us, length us, event | category | flops | bytes accessed | tf_op | source)
XLA Modules:
  0.0 49.9 jit_solution(803152748387896734)
XLA Ops:
  0.6 0.0 copy-start
  0.6 1.1 %copy-done = bf16[640,512]{1,0:T(8,128)(2,1)S(1)} copy-done((bf16[640,512]{1,0:T(8,128)(2,1)S(1)}, bf16[640,512]{1,0:T(8,128)(2,1)}, u32[]{:S(2)}) %copy-start) | copy-done | bytes 655384
  1.7 0.0 copy-start.1
  1.7 0.9 %copy-done.1 = bf16[32,32,128]{2,1,0:T(8,128)(2,1)S(1)} copy-done((bf16[32,32,128]{2,1,0:T(8,128)(2,1)S(1)}, bf16[32,32,128]{2,1,0:T(8,128)(2,1)}, u32[]{:S(2)}) %copy-start.1) | copy-done | bytes 262168
  2.7 0.0 copy-start.2
  2.7 0.9 %copy-done.2 = bf16[32,32,128]{2,1,0:T(8,128)(2,1)S(1)} copy-done((bf16[32,32,128]{2,1,0:T(8,128)(2,1)S(1)}, bf16[32,32,128]{2,1,0:T(8,128)(2,1)}, u32[]{:S(2)}) %copy-start.2) | copy-done | bytes 262168
  3.6 0.0 copy-start.3
  3.6 0.9 %copy-done.3 = bf16[384,128]{1,0:T(8,128)(2,1)S(1)} copy-done((bf16[384,128]{1,0:T(8,128)(2,1)S(1)}, bf16[384,128]{1,0:T(8,128)(2,1)}, u32[]{:S(2)}) %copy-start.3) | copy-done | bytes 98328
  4.5 0.0 copy-start.4
  4.5 0.8 %copy-done.4 = bf16[128,128]{1,0:T(8,128)(2,1)S(1)} copy-done((bf16[128,128]{1,0:T(8,128)(2,1)S(1)}, bf16[128,128]{1,0:T(8,128)(2,1)}, u32[]{:S(2)}) %copy-start.4) | copy-done | bytes 32792
  5.3 0.0 copy-start.5
  5.3 0.7 %copy-done.5 = bf16[48,192]{1,0:T(8,128)(2,1)S(1)} copy-done((bf16[48,192]{1,0:T(8,128)(2,1)S(1)}, bf16[48,192]{1,0:T(8,128)(2,1)}, u32[]{:S(2)}) %copy-start.5) | copy-done | bytes 18456
  6.0 0.0 copy-start.6
  6.0 0.7 %copy-done.6 = s32[1,32,64,1]{2,3,1,0:T(1,128)S(1)} copy-done((s32[1,32,64,1]{2,3,1,0:T(1,128)S(1)}, s32[1,32,64,1]{2,3,1,0:T(1,128)}, u32[]{:S(2)}) %copy-start.6) | copy-done | bytes 8216
  6.7 0.0 copy-start.7
  6.7 0.7 %copy-done.7 = bf16[64,128]{1,0:T(8,128)(2,1)S(1)} copy-done((bf16[64,128]{1,0:T(8,128)(2,1)S(1)}, bf16[64,128]{1,0:T(8,128)(2,1)}, u32[]{:S(2)}) %copy-start.7) | copy-done | bytes 16408
  7.4 0.0 copy-start.8
  7.4 0.7 %copy-done.8 = bf16[32,96]{1,0:T(8,128)(2,1)S(1)} copy-done((bf16[32,96]{1,0:T(8,128)(2,1)S(1)}, bf16[32,96]{1,0:T(8,128)(2,1)}, u32[]{:S(2)}) %copy-start.8) | copy-done | bytes 6168
  8.1 40.6 %shard_map.104 = (f32[3,2,2,9]{3,2,1,0:T(2,128)S(1)}, f32[3,2,2,9]{3,2,1,0:T(2,128)S(1)}) custom-call(bf16[32,32,128]{2,1,0:T(8,128)(2,1)S(1)} %copy-done.1, bf16[32,32,128]{2,1,0:T(8,128)(2,1)S(1)} %copy-done.2, s32[32,1,64]{2,1,0:T(1,128)S(1)} %bitcast.1, bf16[48,192]{1,0:T(8,128)(2,1)S(1)} %copy-done.5, bf16[640,512]{1,0:T(8,128)(2,1)S(1)} %copy-done, ...), custom_call_target="tpu_custom_call" | custom-call | tf_op jit(solution)/shard_map/pallas_call | solution.py:618
  48.7 0.6 %copy.13 = f32[3,2,2,9]{3,2,1,0:T(2,128)} copy(f32[3,2,2,9]{3,2,1,0:T(2,128)S(1)} %get-tuple-element.4) | data formatting | bytes 864
  49.3 0.6 %copy.14 = f32[3,2,2,9]{3,2,1,0:T(2,128)} copy(f32[3,2,2,9]{3,2,1,0:T(2,128)S(1)} %get-tuple-element.5) | data formatting | bytes 864
Async XLA Ops:
  0.6 1.1 %copy-start = (bf16[640,512]{1,0:T(8,128)(2,1)S(1)}, bf16[640,512]{1,0:T(8,128)(2,1)}, u32[]{:S(2)}) copy-start(bf16[640,512]{1,0:T(8,128)(2,1)} %constant.13.clone.wmat_h) | copy-start | bytes 1966084
  1.7 0.9 %copy-start.1 = (bf16[32,32,128]{2,1,0:T(8,128)(2,1)S(1)}, bf16[32,32,128]{2,1,0:T(8,128)(2,1)}, u32[]{:S(2)}) copy-start(bf16[32,32,128]{2,1,0:T(8,128)(2,1)} %ref_h.1) | copy-start | bytes 786436
  2.7 0.9 %copy-start.2 = (bf16[32,32,128]{2,1,0:T(8,128)(2,1)S(1)}, bf16[32,32,128]{2,1,0:T(8,128)(2,1)}, u32[]{:S(2)}) copy-start(bf16[32,32,128]{2,1,0:T(8,128)(2,1)} %def_h.1) | copy-start | bytes 786436
  3.6 0.9 %copy-start.3 = (bf16[384,128]{1,0:T(8,128)(2,1)S(1)}, bf16[384,128]{1,0:T(8,128)(2,1)}, u32[]{:S(2)}) copy-start(bf16[384,128]{1,0:T(8,128)(2,1)} %constant.15.clone.wr_h) | copy-start | bytes 294916
  4.5 0.8 %copy-start.4 = (bf16[128,128]{1,0:T(8,128)(2,1)S(1)}, bf16[128,128]{1,0:T(8,128)(2,1)}, u32[]{:S(2)}) copy-start(bf16[128,128]{1,0:T(8,128)(2,1)} %constant.16.clone.dz_h) | copy-start | bytes 98308
  5.3 0.7 %copy-start.5 = (bf16[48,192]{1,0:T(8,128)(2,1)S(1)}, bf16[48,192]{1,0:T(8,128)(2,1)}, u32[]{:S(2)}) copy-start(bf16[48,192]{1,0:T(8,128)(2,1)} %constant.12.clone.ymat_h) | copy-start | bytes 55300
  6.0 0.7 %copy-start.6 = (s32[1,32,64,1]{2,3,1,0:T(1,128)S(1)}, s32[1,32,64,1]{2,3,1,0:T(1,128)}, u32[]{:S(2)}) copy-start(s32[1,32,64,1]{2,3,1,0:T(1,128)} %param.11) | copy-start | bytes 24580
  6.7 0.7 %copy-start.7 = (bf16[64,128]{1,0:T(8,128)(2,1)S(1)}, bf16[64,128]{1,0:T(8,128)(2,1)}, u32[]{:S(2)}) copy-start(bf16[64,128]{1,0:T(8,128)(2,1)} %constant.17.clone.spread_h) | copy-start | bytes 49156
  7.4 0.7 %copy-start.8 = (bf16[32,96]{1,0:T(8,128)(2,1)S(1)}, bf16[32,96]{1,0:T(8,128)(2,1)}, u32[]{:S(2)}) copy-start(bf16[32,96]{1,0:T(8,128)(2,1)} %constant.14.clone.yr_h) | copy-start | bytes 18436

commit v3 on v2

--- a/solution.py
+++ b/solution.py
@@ -77,7 +77,10 @@
     lanes = np.arange(128)
     spread = (np.arange(64)[:, None] % 4 == lanes[None, :] // 32).astype(np.float64)
     cast = lambda a: a.astype(ml_dtypes.bfloat16)
-    return [cast(a) for a in (ymat, wmat, yr, wr, dz, spread)]
+    both = np.zeros((80, 192))
+    both[:48] = ymat
+    both[48:, :96] = yr
+    return [cast(a) for a in (both, wmat, wr, dz, spread)]
 
 
 def pieces(x):
@@ -115,9 +118,9 @@
 
 
 def kernel(
-    ref_h, def_h, table_h, ymat_h, wmat_h, yr_h, wr_h, dz_h, spread_h,
+    ref_h, def_h, table_h, ys_h, wmat_h, wr_h, dz_h, spread_h,
     upd_out, res_out,
-    table, ymat, yr, wr, dz, spread,
+    table, ys, wr, dz, spread,
     ref_v, own_v, lo_v, hi_v, fs, gs, mask_s, yface, xlo, xhi, ylo, yhi,
     xs, t2, ksend, krecv, rx, rt2, rsend, rrecv, kf, wmat, vsend, vrecv,
     asrc, a1, b1src, b1,
@@ -137,7 +140,7 @@
     load_ref = pltpu.make_async_copy(ref_h, ref_v, lsem.at[0])
     load_own = pltpu.make_async_copy(def_h, own_v, lsem.at[1])
     load_w = pltpu.make_async_copy(wmat_h, wmat, lsem.at[2])
-    small = [(table_h.at[gy], table), (spread_h, spread), (dz_h, dz), (ymat_h, ymat), (yr_h, yr), (wr_h, wr)]
+    small = [(table_h.at[gy], table), (spread_h, spread), (dz_h, dz), (ys_h, ys), (wr_h, wr)]
     small = [pltpu.make_async_copy(src, dst, lsem.at[3 + n]) for n, (src, dst) in enumerate(small)]
     for copy in (load_ref, *small, load_own, load_w):
         copy.start()
@@ -229,10 +232,11 @@
             for u, value in enumerate((a00, a01, a11 + b00, b01, b11)):
                 xs[u, rows, :] = value
 
+    ymat = ys[:48, :]
     t2[40:48, :] = jnp.zeros((8, 640), F32)
     for u in range(5):
         hi, mid, low = pieces(xs[u])
-        t = mm(ymat[...], hi) + mm(ymat[...], mid) + mm(ymat[...], low)
+        t = mm(ymat, hi) + mm(ymat, mid) + mm(ymat, low)
         for m in range(5):
             t2[8 * u : 8 * u + 8, 128 * m : 128 * m + 128] = t[8 * m : 8 * m + 8]
     load_w.wait()
@@ -294,10 +298,11 @@
             rows = slice(c * 32 + 16 * ey, c * 32 + 16 * ey + 16)
             for n, value in enumerate((a0, a1_ + b0, b1_)):
                 rx[n, rows, :] = value
+    yr = ys[48:, :96]
     rt2[24:32, :] = jnp.zeros((8, 384), F32)
     for n in range(3):
         hi, mid, low = pieces(rx[n])
-        t = mm(yr[...], hi) + mm(yr[...], mid) + mm(yr[...], low)
+        t = mm(yr, hi) + mm(yr, mid) + mm(yr, low)
         for m in range(3):
             rt2[8 * n : 8 * n + 8, 128 * m : 128 * m + 128] = t[8 * m : 8 * m + 8]
     stacked = jnp.concatenate(pieces(rt2[...]), axis=0)
@@ -603,7 +608,7 @@
     hbm = pl.BlockSpec(memory_space=pltpu.HBM)
     V, DMA = pltpu.VMEM, pltpu.SemaphoreType.DMA
     scratch = [
-        V((1, 64), jnp.int32), V((48, 192), BF16), V((32, 96), BF16), V((384, 128), BF16), V((128, 128), BF16), V((64, 128), BF16),
+        V((1, 64), jnp.int32), V((80, 192), BF16), V((384, 128), BF16), V((128, 128), BF16), V((64, 128), BF16),
         V((32, 32, 128), BF16), V((32, 32, 128), BF16), V((32, 32, 128), BF16), V((32, 32, 128), BF16),
         V((34, 48, 128), F32), V((3, 32, 32, 128), F32), V((16, 128), F32),
         V((2, 32, 128), BF16), V((32, 128), BF16), V((32, 128), BF16), V((32, 128), BF16), V((32, 128), BF16),
@@ -611,18 +616,18 @@
         V((3, 96, 128), F32), V((32, 384), F32), V((3, 8, 128), F32), V((4, 4, 3, 8, 128), F32),
         V((9, 9, 8, 128), F32), V((640, 512), BF16), V((2, 8, 128), F32), V((3, 3, 2, 8, 128), F32),
         V((2, 8, 128), F32), V((NGY, 2, 8, 128), F32), V((2, 8, 128), F32), V((NGX, 2, 8, 128), F32),
-        DMA((9,)), DMA((6,)), DMA((6,)), DMA((8,)), DMA((8,)), DMA((15,)), DMA((15,)), DMA((8,)), DMA((8,)),
+        DMA((8,)), DMA((6,)), DMA((6,)), DMA((8,)), DMA((8,)), DMA((15,)), DMA((15,)), DMA((8,)), DMA((8,)),
         DMA((2,)), DMA((2,)),
     ]
     out = jax.ShapeDtypeStruct((3, 2, 2, 9), F32)
     return pl.pallas_call(
         kernel,
         out_shape=(out, out),
-        in_specs=[hbm] * 9,
+        in_specs=[hbm] * 8,
         out_specs=(vmem, vmem),
         scratch_shapes=scratch,
         compiler_params=pltpu.CompilerParams(
-            collective_id=0, has_side_effects=True, vmem_limit_bytes=40 * 1024 * 1024
+            collective_id=0, has_side_effects=True, vmem_limit_bytes=55210 * 1024
         ),
     )(reference_scan, deformed_scan, table, *consts)
 

time: 50.4 us -> 42.6 us (0.85)
  local copies, waits for them, and re-layouts: 8.69 us -> 1.19 us
    unnamed x20 -> x2, local copies, waits for them, and re-layouts: 8.69 us -> 1.19 us
where the time goes in v3:
time: 42.6 us; the launch traced here: 42.5 us
  Pallas kernels  40.7 us (96%)
  local copies, waits for them, and re-layouts  1.19 us (3%)
  between operations  0.64 us (2%)
    pallas_call x1, Pallas kernels, local(): pl.pallas_call(kernel, out_shape=(out, out), in_specs=[hbm] * 8, out_spec...  40.7 us
    unnamed x2, local copies, waits for them, and re-layouts  1.19 us

profile of v3, /device:TPU:1, one launch (start us, length us, event | category | flops | bytes accessed | tf_op | source)
XLA Modules:
  0.0 42.5 jit_solution(11831163174824674182)
XLA Ops:
  0.6 40.7 %shard_map.95 = (f32[3,2,2,9]{3,2,1,0:T(2,128)S(1)}, f32[3,2,2,9]{3,2,1,0:T(2,128)S(1)}) custom-call(bf16[32,32,128]{2,1,0:T(8,128)(2,1)} %ref_h.1, bf16[32,32,128]{2,1,0:T(8,128)(2,1)} %def_h.1, s32[32,1,64]{2,1,0:T(1,128)} %bitcast.1, bf16[80,192]{1,0:T(8,128)(2,1)} %constant.10.clone.ys_h, bf16[640,512]{1,0:T(8,128)(2,1)} %constant.11.clone.wmat_h, ...), custom_call_target="tpu_custom_call" | custom-call | tf_op jit(solution)/shard_map/pallas_call | solution.py:623
  41.3 0.6 %copy.12 = f32[3,2,2,9]{3,2,1,0:T(2,128)} copy(f32[3,2,2,9]{3,2,1,0:T(2,128)S(1)} %get-tuple-element.4) | data formatting | bytes 864
  41.9 0.6 %copy.13 = f32[3,2,2,9]{3,2,1,0:T(2,128)} copy(f32[3,2,2,9]{3,2,1,0:T(2,128)S(1)} %get-tuple-element.5) | data formatting | bytes 864

commit v4 on v3

--- a/solution.py
+++ b/solution.py
@@ -18,6 +18,10 @@
 
 NEIGHBOURS = [(dx, dy) for dx in (-1, 0, 1) for dy in (-1, 0, 1) if (dx, dy) != (0, 0)]
 SOURCES = [(bx, by) for bx in (-2, -1, 0, 1) for by in (-2, -1, 0, 1) if (bx, by) != (0, 0)]
+SOURCES.sort(key=lambda b: -abs(b[0]) - 0.9 * abs(b[1]))
+NEIGHBOURS.sort(key=lambda b: -abs(b[0]) - abs(b[1]))
+FAR_Y = sorted(range(1, NGY), key=lambda m: -min(m // 8, 4 - m // 8) - min(m % 8, 8 - m % 8) / 2)
+FAR_X = sorted(range(1, NGX), key=lambda m: -min(m, NGX - m))
 PAIRS = [(0, 0), (1, 1), (2, 2), (0, 1), (1, 2), (2, 0)]
 
 
@@ -66,7 +70,7 @@
             yr[n * 8 + r, c * 32 : (c + 1) * 32] = wy[n] / 32.0
     wr = np.zeros((3, 128, 8, 16))
     for n in range(3):
-        wr[n, :, 2 + n, :9] = wz.T
+        wr[n, :, n, :9] = wr[n, :, 4 + n, :9] = wz.T
     wr = wr.reshape(384, 128)
     dz = np.zeros((128, 128))
     for z in range(128):
@@ -121,28 +125,33 @@
     ref_h, def_h, table_h, ys_h, wmat_h, wr_h, dz_h, spread_h,
     upd_out, res_out,
     table, ys, wr, dz, spread,
-    ref_v, own_v, lo_v, hi_v, fs, gs, mask_s, yface, xlo, xhi, ylo, yhi,
+    ref_v, own_v, def_v, fs, gs, mask_s, yface, faces,
     xs, t2, ksend, krecv, rx, rt2, rsend, rrecv, kf, wmat, vsend, vrecv,
     asrc, a1, b1src, b1,
-    lsem, fsend, frecv, ksem_s, ksem_r, rsem_s, rsem_r, vsem_s, vsem_r, arsem_s, arsem_r,
+    ktotal, lsem, sems,
 ):
     gx, gy = lax.axis_index("gx"), lax.axis_index("gy")
 
+    gx_at = [lax.rem(gx + d, NGX) for d in range(NGX)]
+    gy_at = [lax.rem(gy + d, NGY) for d in range(NGY)]
+
     def at(dx, dy):
-        return (lax.rem(gx + (dx + NGX), NGX), lax.rem(gy + (dy + NGY), NGY))
-
-    barrier = pltpu.get_barrier_semaphore()
-    partners = [at(0, m) for m in range(1, NGY)] + [at(m, 0) for m in range(1, NGX)]
-    partners += [at(bx, by) for bx, by in SOURCES if bx != 0 and by != 0]
-    for partner in partners:
-        pl.semaphore_signal(barrier, inc=1, device_id=partner, device_id_type=MESH)
+        return (gx_at[dx % NGX], gy_at[dy % NGY])
 
     load_ref = pltpu.make_async_copy(ref_h, ref_v, lsem.at[0])
     load_own = pltpu.make_async_copy(def_h, own_v, lsem.at[1])
     load_w = pltpu.make_async_copy(wmat_h, wmat, lsem.at[2])
     small = [(table_h.at[gy], table), (spread_h, spread), (dz_h, dz), (ys_h, ys), (wr_h, wr)]
     small = [pltpu.make_async_copy(src, dst, lsem.at[3 + n]) for n, (src, dst) in enumerate(small)]
-    for copy in (load_ref, *small, load_own, load_w):
+    load_ref.start()
+
+    barrier = pltpu.get_barrier_semaphore()
+    partners = [at(0, 1), at(0, -1), at(1, 0), at(-1, 0)]
+    partners += [at(bx, by) for bx, by in SOURCES if bx != 0 and by != 0]
+    partners += [at(0, m) for m in range(2, NGY - 1)] + [at(m, 0) for m in range(2, NGX - 1)]
+    for partner in partners:
+        pl.semaphore_signal(barrier, inc=1, device_id=partner, device_id_type=MESH)
+    for copy in (*small, load_own, load_w):
         copy.start()
 
     def flag(condition):
@@ -151,6 +160,26 @@
     xlo_ok, xhi_ok = flag(gx > 0), flag(gx < NGX - 1)
     ylo_ok, yhi_ok = flag(gy > 0), flag(gy < NGY - 1)
 
+    load_ref.wait()
+    yface[0] = jnp.concatenate([ref_v[x, 24:32, :].astype(F32)[7:8] for x in range(32)], axis=0).astype(BF16)
+    yface[1] = jnp.concatenate([ref_v[x, 0:8, :].astype(F32)[0:1] for x in range(32)], axis=0).astype(BF16)
+
+    pl.semaphore_wait(barrier, len(partners))
+
+    def send(src, dst, s, r, to):
+        pltpu.make_async_remote_copy(
+            src_ref=src, dst_ref=dst, send_sem=s, recv_sem=r, device_id=to, device_id_type=MESH
+        ).start()
+
+    def wait(as_much, sem):
+        pltpu.make_async_copy(as_much, as_much, sem).wait()
+
+    send(yface.at[0], faces.at[0], sems.at[0, 0], sems.at[0, 1], at(0, 1))
+    send(yface.at[1], faces.at[1], sems.at[0, 0], sems.at[0, 1], at(0, -1))
+    send(ref_h.at[31], faces.at[2], sems.at[0, 0], sems.at[0, 1], at(1, 0))
+    send(ref_h.at[0], faces.at[3], sems.at[0, 0], sems.at[0, 1], at(-1, 0))
+    send(def_h, def_v.at[0], sems.at[1, 0], sems.at[1, 1], at(0, 1))
+    send(def_h, def_v.at[1], sems.at[1, 0], sems.at[1, 1], at(0, -1))
     for copy in small:
         copy.wait()
     row = (table[...] - gy).astype(F32)
@@ -159,38 +188,15 @@
     picked = jnp.where(c64 // 4 == r16, jnp.broadcast_to(row, (16, 64)), 0.0).astype(BF16)
     mask_s[...] = mm(picked, spread[...])
 
-    load_ref.wait()
     for x in range(32):
         plane = ref_v[x]
         fs[x + 1, 8:40, :] = plane.astype(F32)
         gs[2, x] = mm(plane, dz[...])
-    yface[0] = jnp.concatenate([fs[x + 1, 39:40, :] for x in range(32)], axis=0).astype(BF16)
-    yface[1] = jnp.concatenate([fs[x + 1, 8:9, :] for x in range(32)], axis=0).astype(BF16)
-
-    pl.semaphore_wait(barrier, len(partners))
-
-    def send(src, dst, s, r, to):
-        copy = pltpu.make_async_remote_copy(
-            src_ref=src, dst_ref=dst, send_sem=s, recv_sem=r, device_id=to, device_id_type=MESH
-        )
-        copy.start()
-        return copy
-
-    c_ylo = send(yface.at[0], ylo, fsend.at[0], frecv.at[0], at(0, 1))
-    c_yhi = send(yface.at[1], yhi, fsend.at[1], frecv.at[1], at(0, -1))
-    c_xlo = send(ref_v.at[31], xlo, fsend.at[2], frecv.at[2], at(1, 0))
-    c_xhi = send(ref_v.at[0], xhi, fsend.at[3], frecv.at[3], at(-1, 0))
-    load_own.wait()
-    c_dlo = send(own_v, lo_v, fsend.at[4], frecv.at[4], at(0, 1))
-    c_dhi = send(own_v, hi_v, fsend.at[5], frecv.at[5], at(0, -1))
-    c_xlo.wait_recv()
-    c_xhi.wait_recv()
-    c_ylo.wait_recv()
-    c_yhi.wait_recv()
-    fs[0, 8:40, :] = xlo[...].astype(F32) * xlo_ok
-    fs[33, 8:40, :] = xhi[...].astype(F32) * xhi_ok
-    face_lo = ylo[...].astype(F32) * ylo_ok
-    face_hi = yhi[...].astype(F32) * yhi_ok
+    wait(faces, sems.at[0, 1])
+    fs[0, 8:40, :] = faces[2].astype(F32) * xlo_ok
+    fs[33, 8:40, :] = faces[3].astype(F32) * xhi_ok
+    face_lo = faces[0].astype(F32) * ylo_ok
+    face_hi = faces[1].astype(F32) * yhi_ok
     for x in range(32):
         fs[x + 1, 7:8, :] = face_lo[x : x + 1]
         fs[x + 1, 40:41, :] = face_hi[x : x + 1]
@@ -232,38 +238,11 @@
             for u, value in enumerate((a00, a01, a11 + b00, b01, b11)):
                 xs[u, rows, :] = value
 
-    ymat = ys[:48, :]
-    t2[40:48, :] = jnp.zeros((8, 640), F32)
-    for u in range(5):
-        hi, mid, low = pieces(xs[u])
-        t = mm(ymat, hi) + mm(ymat, mid) + mm(ymat, low)
-        for m in range(5):
-            t2[8 * u : 8 * u + 8, 128 * m : 128 * m + 128] = t[8 * m : 8 * m + 8]
-    load_w.wait()
-    stacked = jnp.concatenate(pieces(t2[...]), axis=0)
-    done = mm(stacked, wmat[...])
-    done = done[:48] + done[48:96] + done[96:144]
-    for u in range(5):
-        for group in range(4):
-            ksend[group, u] = done[8 * u : 8 * u + 8, 128 * group : 128 * group + 128]
-
-    GROUP = {1: (0, 1), 0: (1, 2), -1: (3, 1)}
-    UNIT = {1: (1, 4), 0: (0, 5), -1: (0, 2)}
-    kcopies = []
-    for n, (dx, dy) in enumerate(NEIGHBOURS):
-        g0, gn = GROUP[dy]
-        u0, un = UNIT[dx]
-        kcopies.append(
-            send(
-                ksend.at[pl.ds(g0, gn), pl.ds(u0, un)],
-                krecv.at[1 - dx, pl.ds(g0, gn), pl.ds(u0, un)],
-                ksem_s.at[n], ksem_r.at[n], at(dx, dy),
-            )
-        )
-    krecv[1, 1:3] = ksend[1:3]
-
-    c_dlo.wait_recv()
-    c_dhi.wait_recv()
+    lane = lax.broadcasted_iota(jnp.int32, (8, 128), 1)
+    sub = lax.broadcasted_iota(jnp.int32, (8, 128), 0)
+
+    load_own.wait()
+    wait(def_v, sems.at[1, 1])
     for ey in range(2):
         r = 8 + 16 * ey
         y = slice(16 * ey, 16 * ey + 16)
@@ -280,8 +259,8 @@
                 def step(t, carry, below=below, above=above, ex=ex, xb=xb, r=r, y=y):
                     x = 16 * ex + 8 * xb + t
                     warped = jnp.where(
-                        below, lo_v[x, y, :].astype(F32),
-                        jnp.where(above, hi_v[x, y, :].astype(F32), own_v[x, y, :].astype(F32)),
+                        below, def_v[0, x, y, :].astype(F32),
+                        jnp.where(above, def_v[1, x, y, :].astype(F32), own_v[x, y, :].astype(F32)),
                     )
                     misfit = fs[x + 1, r : r + 16, :] - warped
                     out = []
@@ -308,25 +287,45 @@
     stacked = jnp.concatenate(pieces(rt2[...]), axis=0)
     done = mm(stacked, wr[...])
     done = done[:32] + done[32:64] + done[64:96]
-    for n in range(3):
-        rsend[n] = done[8 * n : 8 * n + 8]
-    rcopies = []
-    for n, (bx, by) in enumerate(SOURCES):
-        rcopies.append(
-            send(rsend, rrecv.at[bx + 2, by + 2], rsem_s.at[n], rsem_r.at[n], at(-bx, -by))
+    rsend[...] = jnp.where(lane < 64, jnp.where(sub < 3, done[:8], done[8:16]), done[16:24])
+    for bx, by in SOURCES:
+        send(rsend, rrecv.at[4 * bx + by + 10], sems.at[3, 0], sems.at[3, 1], at(-bx, -by))
+    rrecv[10] = rsend[...]
+
+    ymat = ys[:48, :]
+    t2[40:48, :] = jnp.zeros((8, 640), F32)
+    for u in range(5):
+        hi, mid, low = pieces(xs[u])
+        t = mm(ymat, hi) + mm(ymat, mid) + mm(ymat, low)
+        for m in range(5):
+            t2[8 * u : 8 * u + 8, 128 * m : 128 * m + 128] = t[8 * m : 8 * m + 8]
+    load_w.wait()
+    stacked = jnp.concatenate(pieces(t2[...]), axis=0)
+    done = mm(stacked, wmat[...])
+    done = done[:48] + done[48:96] + done[96:144]
+    for u in range(5):
+        for group in range(4):
+            ksend[group, u] = done[8 * u : 8 * u + 8, 128 * group : 128 * group + 128]
+
+    GROUP = {1: (0, 1), 0: (1, 2), -1: (3, 1)}
+    UNIT = {1: (1, 4), 0: (0, 5), -1: (0, 2)}
+    for dx, dy in NEIGHBOURS:
+        g0, gn = GROUP[dy]
+        u0, un = UNIT[dx]
+        send(
+            ksend.at[pl.ds(g0, gn), pl.ds(u0, un)],
+            krecv.at[1 - dx, pl.ds(g0, gn), pl.ds(u0, un)],
+            sems.at[2, 0], sems.at[2, 1], at(dx, dy),
         )
-    rrecv[2, 2] = rsend[...]
-
-    lane = lax.broadcasted_iota(jnp.int32, (8, 128), 1)
-    sub = lax.broadcasted_iota(jnp.int32, (8, 128), 0)
+    krecv[1, 1:3] = ksend[1:3]
+
     slot, depth = lane // 16, lane % 16
 
     def roll(x, shift):
         shift = shift % 128
         return x if shift == 0 else pltpu.roll(x, shift, 1)
 
-    for copy in kcopies:
-        copy.wait_recv()
+    wait(ktotal, sems.at[2, 1])
     in_a_diag = jnp.where(slot == 1, 1.0, jnp.where(slot == 2, ylo_ok, 0.0))
     in_b_diag = (slot >= 2) & (slot <= 4)
     for e in range(9):
@@ -393,47 +392,51 @@
             out[i] = jnp.where(sub < 3, total, jnp.where(sub < 6, pltpu.roll(total, 3, 0), pltpu.roll(total, 6, 0)))
         return out
 
-    for copy in rcopies:
-        copy.wait_recv()
+    wait(rrecv.at[pl.ds(0, 15)], sems.at[3, 1])
     w0 = {}
     lo2_x, lo2_y = flag(gx > 1), flag(gy > 1)
     x_ok = {-2: lo2_x, -1: xlo_ok, 0: None, 1: None}
     y_ok = {-2: lo2_y, -1: ylo_ok, 0: None, 1: None}
-    for i in range(-2, 4):
-        total = None
-        for by in (-2, -1, 0, 1):
-            part = None
-            for bx in (-2, -1, 0, 1):
-                n = i - 2 * bx
-                if 0 <= n <= 2:
-                    term = rrecv[bx + 2, by + 2, n]
-                    if x_ok[bx] is not None:
-                        term = term * x_ok[bx]
-                    part = term if part is None else part + term
-            part = roll(part, 32 * by)
+    totals = {i: None for i in range(-2, 4)}
+    for by in (-2, -1, 0, 1):
+        part = {i: None for i in range(-2, 4)}
+        for bx in (-2, -1, 0, 1):
+            tile = rrecv[4 * bx + by + 10]
+            if x_ok[bx] is not None:
+                tile = tile * x_ok[bx]
+            for n in range(3):
+                i = 2 * bx + n
+                if i in part:
+                    shifted = (tile, pltpu.roll(tile, 5, 0), roll(tile, 64))[n]
+                    part[i] = add(part[i], shifted)
+        for i in part:
+            here = jnp.where(lane < 48, part[i], 0.0)
             if y_ok[by] is not None:
-                part = part * y_ok[by]
-            total = part if total is None else total + part
-        w0[i] = total * node_mask[i]
+                here = here * y_ok[by]
+            totals[i] = add(totals[i], roll(here, 32 * (by + 1)))
+    for i in totals:
+        t = totals[i]
+        t = jnp.where(sub < 3, t, jnp.where(sub < 6, pltpu.roll(t, 3, 0), pltpu.roll(t, 6, 0)))
+        w0[i] = t * node_mask[i]
 
     w1 = apply(w0, (-1, 0, 1, 2))
     w1 = {i: w1[i] * node_mask[i] for i in w1}
     w2_own = apply(w1, (0, 1))
-    for i in range(2):
-        vsend[i] = w2_own[i] * own_mask
-    vcopies = []
-    for n, (dx, dy) in enumerate(NEIGHBOURS):
-        vcopies.append(
-            send(vsend, vrecv.at[1 - dx, 1 - dy], vsem_s.at[n], vsem_r.at[n], at(dx, dy))
-        )
-    vrecv[1, 1] = vsend[...]
-
-    for copy in vcopies:
-        copy.wait_recv()
+    vsend[...] = jnp.where(sub < 3, w2_own[0], w2_own[1]) * own_mask
+    for dx, dy in NEIGHBOURS:
+        send(vsend, vrecv.at[4 - 3 * dx - dy], sems.at[4, 0], sems.at[4, 1], at(dx, dy))
+    vrecv[4] = vsend[...]
+
+    wait(vrecv.at[pl.ds(0, 8)], sems.at[4, 1])
     w2 = {}
     for i in range(-2, 4):
-        bx, n = i // 2, i % 2
-        total = vrecv[bx + 1, 1, n] + roll(vrecv[bx + 1, 0, n], -32) + roll(vrecv[bx + 1, 2, n], 32)
+        if i % 2 == 0:
+            b = 3 * (i // 2) + 4
+            t = vrecv[b] + roll(vrecv[b - 1], -32) + roll(vrecv[b + 1], 32)
+            back, ahead = pltpu.roll(t, 5, 0), pltpu.roll(t, 3, 0)
+            total = jnp.where(sub < 3, t, jnp.where(sub < 6, ahead, pltpu.roll(t, 6, 0)))
+        else:
+            total = jnp.where(sub < 3, back, jnp.where(sub < 6, t, ahead))
         w2[i] = total * node_mask[i]
     w3 = apply(w2, (-1, 0, 1, 2))
     w3 = {i: w3[i] * node_mask[i] for i in w3}
@@ -454,33 +457,38 @@
         value = jnp.where(sub == j, p, value)
         remainder = jnp.where(sub == j, e, remainder)
 
-    def pair_tree(slots):
-        p, e = slots[:, 0], slots[:, 1]
+    for shift in (16, 8, 4, 2, 1):
+        remainder = remainder + roll(remainder, -shift)
+        value, err = two_sum(value, roll(value, -shift))
+        remainder = remainder + err
+    line = jnp.zeros((1, 128), F32)
+    first = (lane % 32 == 0)[:1]
+    for j in range(5):
+        line = line + roll(jnp.where(first, value[j : j + 1], 0.0), j)
+        line = line + roll(jnp.where(first, remainder[j : j + 1], 0.0), 8 + j)
+
+    def line_tree(slots):
+        p, e = slots, None
         while p.shape[0] > 1:
             half = p.shape[0] // 2
-            e = e[:half] + e[half:]
             p, err = two_sum(p[:half], p[half:])
-            e = e + err
+            e = err if e is None else e[:half] + e[half:] + err
         return p[0], e[0]
 
-    asrc[0] = value
-    asrc[1] = remainder
-    a1[gy] = asrc[...]
-    for m in range(1, NGY):
-        send(asrc, a1.at[gy], arsem_s.at[0], arsem_r.at[0], at(0, m))
-    pltpu.make_async_copy(a1.at[pl.ds(0, NGY - 1)], a1.at[pl.ds(0, NGY - 1)], arsem_r.at[0]).wait()
-    p, e = pair_tree(a1[...])
-    b1src[0] = p
-    b1src[1] = e
-    b1[gx] = b1src[...]
-    for m in range(1, NGX):
-        send(b1src, b1.at[gx], arsem_s.at[1], arsem_r.at[1], at(m, 0))
-    pltpu.make_async_copy(b1.at[pl.ds(0, NGX - 1)], b1.at[pl.ds(0, NGX - 1)], arsem_r.at[1]).wait()
-    p, e = pair_tree(b1[...])
-    for shift in (16, 8, 4, 2, 1):
-        e = e + roll(e, -shift)
-        p, err = two_sum(p, roll(p, -shift))
-        e = e + err
+    asrc[...] = line
+    a1[gy] = line
+    for m in FAR_Y:
+        send(asrc, a1.at[gy], sems.at[5, 0], sems.at[5, 1], at(0, m))
+    wait(a1.at[pl.ds(0, NGY - 1)], sems.at[5, 1])
+    p, e = line_tree(a1[...])
+    line = jnp.where((lane % 16 < 8)[:1], p, p + roll(e, 8))
+    b1src[...] = line
+    b1[gx] = line
+    for m in FAR_X:
+        send(b1src, b1.at[gx], sems.at[6, 0], sems.at[6, 1], at(m, 0))
+    wait(b1.at[pl.ds(0, NGX - 1)], sems.at[6, 1])
+    p, e = line_tree(b1[...])
+    e = e + roll(p, -8)
     high = p + e
     low = (p - high) + e
 
@@ -488,7 +496,7 @@
         t = x * 262145.0
         return t - (t - x)
 
-    m0, m1, m2 = high[0:1, 0:1], high[1:2, 0:1], high[1:2, 32:33]
+    m0, m1, m2 = [jnp.broadcast_to(high[:, n : n + 1], (8, 128)) for n in (0, 1, 33)]
     mean = m1 / m0
     mu = few_bits(mean)
     spread_q = few_bits(jnp.maximum(m2 / m0 - mean * mean, 1e-5 * mean * mean))
@@ -505,7 +513,7 @@
     def combine(coefficients, terms):
         total = None
         for c, (h, l) in zip(coefficients, terms):
-            c = jnp.broadcast_to(c, h.shape)
+            c = c[: h.shape[0]]
             p, e = two_prod(c, split(c), h, split(h))
             e = e + c * l
             if total is None:
@@ -516,7 +524,7 @@
         h = total[0] + total[1]
         return h, (total[0] - h) + total[1]
 
-    rows_w = [(high[j : j + 1], low[j : j + 1]) for j in range(5)]
+    rows_w = [(roll(high, -j), roll(low, -j)) for j in range(5)]
     rows_q = [combine(poly[k], rows_w) for k in range(5)]
     filler = [jnp.zeros((3, 128), F32)]
     mixed = [jnp.concatenate([r[n] for r in rows_q] + filler, axis=0) for n in range(2)]
@@ -525,7 +533,7 @@
     for l in range(4):
         h, _ = combine(poly[l], moved)
         for k in range(l, 5):
-            G[k, l] = G[l, k] = h[k : k + 1, 0:1]
+            G[k, l] = G[l, k] = jnp.broadcast_to(h[k : k + 1, 0:1], (8, 128))
 
     own = (0, 1)
 
@@ -595,10 +603,9 @@
                 for c in range(3):
                     out[c, i, j : j + 1, :] = moved[c : c + 1, :9]
 
-    for copy in (c_ylo, c_yhi, c_xlo, c_xhi, c_dlo, c_dhi, *kcopies, *rcopies, *vcopies):
-        copy.wait_send()
-    pltpu.make_async_copy(a1.at[pl.ds(0, NGY - 1)], a1.at[pl.ds(0, NGY - 1)], arsem_s.at[0]).wait()
-    pltpu.make_async_copy(b1.at[pl.ds(0, NGX - 1)], b1.at[pl.ds(0, NGX - 1)], arsem_s.at[1]).wait()
+    sent = (faces, def_v, ktotal, rrecv.at[pl.ds(0, 15)], vrecv.at[pl.ds(0, 8)], a1.at[pl.ds(0, NGY - 1)], b1.at[pl.ds(0, NGX - 1)])
+    for n, as_much in enumerate(sent):
+        wait(as_much, sems.at[n, 0])
 
 
 def local(reference_scan, deformed_scan, source_column):
@@ -609,15 +616,14 @@
     V, DMA = pltpu.VMEM, pltpu.SemaphoreType.DMA
     scratch = [
         V((1, 64), jnp.int32), V((80, 192), BF16), V((384, 128), BF16), V((128, 128), BF16), V((64, 128), BF16),
-        V((32, 32, 128), BF16), V((32, 32, 128), BF16), V((32, 32, 128), BF16), V((32, 32, 128), BF16),
+        V((32, 32, 128), BF16), V((32, 32, 128), BF16), V((2, 32, 32, 128), BF16),
         V((34, 48, 128), F32), V((3, 32, 32, 128), F32), V((16, 128), F32),
-        V((2, 32, 128), BF16), V((32, 128), BF16), V((32, 128), BF16), V((32, 128), BF16), V((32, 128), BF16),
+        V((2, 32, 128), BF16), V((4, 32, 128), BF16),
         V((5, 192, 128), F32), V((48, 640), F32), V((4, 5, 8, 128), F32), V((3, 4, 5, 8, 128), F32),
-        V((3, 96, 128), F32), V((32, 384), F32), V((3, 8, 128), F32), V((4, 4, 3, 8, 128), F32),
-        V((9, 9, 8, 128), F32), V((640, 512), BF16), V((2, 8, 128), F32), V((3, 3, 2, 8, 128), F32),
-        V((2, 8, 128), F32), V((NGY, 2, 8, 128), F32), V((2, 8, 128), F32), V((NGX, 2, 8, 128), F32),
-        DMA((8,)), DMA((6,)), DMA((6,)), DMA((8,)), DMA((8,)), DMA((15,)), DMA((15,)), DMA((8,)), DMA((8,)),
-        DMA((2,)), DMA((2,)),
+        V((3, 96, 128), F32), V((32, 384), F32), V((8, 128), F32), V((16, 8, 128), F32),
+        V((9, 9, 8, 128), F32), V((640, 512), BF16), V((8, 128), F32), V((9, 8, 128), F32),
+        V((1, 128), F32), V((NGY, 1, 128), F32), V((1, 128), F32), V((NGX, 1, 128), F32),
+        V((34, 8, 128), F32), DMA((8,)), DMA((7, 2)),
     ]
     out = jax.ShapeDtypeStruct((3, 2, 2, 9), F32)
     return pl.pallas_call(

time: 42.6 us -> 40.9 us (0.960)
  Pallas kernels: 40.7 us -> 38.9 us
    pallas_call x1, Pallas kernels: 40.7 us -> 38.9 us  [local(): pl.pallas_call(kernel, out_shape=(out, out), in_specs=[hbm] * 8, out_spec...]
where the time goes in v4:
time: 40.9 us; the launch traced here: 40.8 us
  Pallas kernels  38.9 us (95%)
  local copies, waits for them, and re-layouts  1.19 us (3%)
  between operations  0.64 us (2%)
    pallas_call x1, Pallas kernels, local(): pl.pallas_call(kernel, out_shape=(out, out), in_specs=[hbm] * 8, out_spec...  38.9 us
    unnamed x2, local copies, waits for them, and re-layouts  1.19 us

profile of v4, /device:TPU:1, one launch (start us, length us, event | category | flops | bytes accessed | tf_op | source)
XLA Modules:
  0.0 40.8 jit_solution(18405918715780928180)
XLA Ops:
  0.6 38.9 %shard_map.95 = (f32[3,2,2,9]{3,2,1,0:T(2,128)S(1)}, f32[3,2,2,9]{3,2,1,0:T(2,128)S(1)}) custom-call(bf16[32,32,128]{2,1,0:T(8,128)(2,1)} %ref_h.1, bf16[32,32,128]{2,1,0:T(8,128)(2,1)} %def_h.1, s32[32,1,64]{2,1,0:T(1,128)} %bitcast.1, bf16[80,192]{1,0:T(8,128)(2,1)} %constant.10.clone.ys_h, bf16[640,512]{1,0:T(8,128)(2,1)} %constant.11.clone.wmat_h, ...), custom_call_target="tpu_custom_call" | custom-call | tf_op jit(solution)/shard_map/pallas_call | solution.py:629
  39.6 0.6 %copy.12 = f32[3,2,2,9]{3,2,1,0:T(2,128)} copy(f32[3,2,2,9]{3,2,1,0:T(2,128)S(1)} %get-tuple-element.4) | data formatting | bytes 864
  40.2 0.6 %copy.13 = f32[3,2,2,9]{3,2,1,0:T(2,128)} copy(f32[3,2,2,9]{3,2,1,0:T(2,128)S(1)} %get-tuple-element.5) | data formatting | bytes 864

commit v5 on v4

--- a/solution.py
+++ b/solution.py
@@ -123,7 +123,7 @@
 
 def kernel(
     ref_h, def_h, table_h, ys_h, wmat_h, wr_h, dz_h, spread_h,
-    upd_out, res_out,
+    out_ref,
     table, ys, wr, dz, spread,
     ref_v, own_v, def_v, fs, gs, mask_s, yface, faces,
     xs, t2, ksend, krecv, rx, rt2, rsend, rrecv, kf, wmat, vsend, vrecv,
@@ -176,10 +176,13 @@
 
     send(yface.at[0], faces.at[0], sems.at[0, 0], sems.at[0, 1], at(0, 1))
     send(yface.at[1], faces.at[1], sems.at[0, 0], sems.at[0, 1], at(0, -1))
-    send(ref_h.at[31], faces.at[2], sems.at[0, 0], sems.at[0, 1], at(1, 0))
-    send(ref_h.at[0], faces.at[3], sems.at[0, 0], sems.at[0, 1], at(-1, 0))
-    send(def_h, def_v.at[0], sems.at[1, 0], sems.at[1, 1], at(0, 1))
-    send(def_h, def_v.at[1], sems.at[1, 0], sems.at[1, 1], at(0, -1))
+    send(ref_v.at[31], faces.at[2], sems.at[0, 0], sems.at[0, 1], at(1, 0))
+    send(ref_v.at[0], faces.at[3], sems.at[0, 0], sems.at[0, 1], at(-1, 0))
+    load_own.wait()
+    for part in range(2):
+        rows = pl.ds(16 * part, 16)
+        for side, dy in ((0, 1), (1, -1)):
+            send(own_v.at[rows], def_v.at[side, rows], sems.at[1, 0], sems.at[(1, 7)[part], 1], at(0, dy))
     for copy in small:
         copy.wait()
     row = (table[...] - gy).astype(F32)
@@ -238,16 +241,42 @@
             for u, value in enumerate((a00, a01, a11 + b00, b01, b11)):
                 xs[u, rows, :] = value
 
+    ymat = ys[:48, :]
+    t2[40:48, :] = jnp.zeros((8, 640), F32)
+    for u in range(5):
+        hi, mid, low = pieces(xs[u])
+        t = mm(ymat, hi) + mm(ymat, mid) + mm(ymat, low)
+        for m in range(5):
+            t2[8 * u : 8 * u + 8, 128 * m : 128 * m + 128] = t[8 * m : 8 * m + 8]
+    load_w.wait()
+    stacked = jnp.concatenate(pieces(t2[...]), axis=0)
+    done = mm(stacked, wmat[...])
+    done = done[:48] + done[48:96] + done[96:144]
+    for u in range(5):
+        for group in range(4):
+            ksend[group, u] = done[8 * u : 8 * u + 8, 128 * group : 128 * group + 128]
+
+    GROUP = {1: (0, 1), 0: (1, 2), -1: (3, 1)}
+    UNIT = {1: (1, 4), 0: (0, 5), -1: (0, 2)}
+    for dx, dy in NEIGHBOURS:
+        g0, gn = GROUP[dy]
+        u0, un = UNIT[dx]
+        send(
+            ksend.at[pl.ds(g0, gn), pl.ds(u0, un)],
+            krecv.at[1 - dx, pl.ds(g0, gn), pl.ds(u0, un)],
+            sems.at[2, 0], sems.at[2, 1], at(dx, dy),
+        )
+    krecv[1, 1:3] = ksend[1:3]
+
     lane = lax.broadcasted_iota(jnp.int32, (8, 128), 1)
     sub = lax.broadcasted_iota(jnp.int32, (8, 128), 0)
 
-    load_own.wait()
-    wait(def_v, sems.at[1, 1])
-    for ey in range(2):
-        r = 8 + 16 * ey
-        y = slice(16 * ey, 16 * ey + 16)
-        parts = []
-        for ex in range(2):
+    parts = {}
+    for ex in range(2):
+        wait(def_v.at[:, pl.ds(16 * ex, 16)], sems.at[(1, 7)[ex], 1])
+        for ey in range(2):
+            r = 8 + 16 * ey
+            y = slice(16 * ey, 16 * ey + 16)
             carry = tuple((jnp.zeros((16, 128), F32),) * 2 for _ in range(3))
             for xb in range(2):
                 k = (2 * ex + xb) * 4 + 2 * ey
@@ -271,9 +300,10 @@
                     return tuple(out)
 
                 carry = lax.fori_loop(0, 8, step, carry, unroll=4)
-            parts.append([(s2 * (1.0 / 16.0), s1 - s2 * (1.0 / 16.0)) for s1, s2 in carry])
+            parts[ex, ey] = [(s2 * (1.0 / 16.0), s1 - s2 * (1.0 / 16.0)) for s1, s2 in carry]
+    for ey in range(2):
         for c in range(3):
-            (a0, a1_), (b0, b1_) = parts[0][c], parts[1][c]
+            (a0, a1_), (b0, b1_) = parts[0, ey][c], parts[1, ey][c]
             rows = slice(c * 32 + 16 * ey, c * 32 + 16 * ey + 16)
             for n, value in enumerate((a0, a1_ + b0, b1_)):
                 rx[n, rows, :] = value
@@ -291,33 +321,6 @@
     for bx, by in SOURCES:
         send(rsend, rrecv.at[4 * bx + by + 10], sems.at[3, 0], sems.at[3, 1], at(-bx, -by))
     rrecv[10] = rsend[...]
-
-    ymat = ys[:48, :]
-    t2[40:48, :] = jnp.zeros((8, 640), F32)
-    for u in range(5):
-        hi, mid, low = pieces(xs[u])
-        t = mm(ymat, hi) + mm(ymat, mid) + mm(ymat, low)
-        for m in range(5):
-            t2[8 * u : 8 * u + 8, 128 * m : 128 * m + 128] = t[8 * m : 8 * m + 8]
-    load_w.wait()
-    stacked = jnp.concatenate(pieces(t2[...]), axis=0)
-    done = mm(stacked, wmat[...])
-    done = done[:48] + done[48:96] + done[96:144]
-    for u in range(5):
-        for group in range(4):
-            ksend[group, u] = done[8 * u : 8 * u + 8, 128 * group : 128 * group + 128]
-
-    GROUP = {1: (0, 1), 0: (1, 2), -1: (3, 1)}
-    UNIT = {1: (1, 4), 0: (0, 5), -1: (0, 2)}
-    for dx, dy in NEIGHBOURS:
-        g0, gn = GROUP[dy]
-        u0, un = UNIT[dx]
-        send(
-            ksend.at[pl.ds(g0, gn), pl.ds(u0, un)],
-            krecv.at[1 - dx, pl.ds(g0, gn), pl.ds(u0, un)],
-            sems.at[2, 0], sems.at[2, 1], at(dx, dy),
-        )
-    krecv[1, 1:3] = ksend[1:3]
 
     slot, depth = lane // 16, lane % 16
 
@@ -591,7 +594,7 @@
             beta = new / rr
             direction = [add(r, None if d is None else beta * d) for r, d in zip(residual, direction)]
             rr = new
-    for coords, out in ((update, upd_out), (residual, res_out)):
+    for first_row, coords in ((0, update), (3, residual)):
         for i in range(2):
             total = None
             for k in range(5):
@@ -601,7 +604,7 @@
             for j in range(2):
                 moved = roll(total, -(32 + 16 * j))
                 for c in range(3):
-                    out[c, i, j : j + 1, :] = moved[c : c + 1, :9]
+                    out_ref[first_row + c, i, j : j + 1, :] = moved[c : c + 1, :9]
 
     sent = (faces, def_v, ktotal, rrecv.at[pl.ds(0, 15)], vrecv.at[pl.ds(0, 8)], a1.at[pl.ds(0, NGY - 1)], b1.at[pl.ds(0, NGX - 1)])
     for n, as_much in enumerate(sent):
@@ -623,19 +626,19 @@
         V((3, 96, 128), F32), V((32, 384), F32), V((8, 128), F32), V((16, 8, 128), F32),
         V((9, 9, 8, 128), F32), V((640, 512), BF16), V((8, 128), F32), V((9, 8, 128), F32),
         V((1, 128), F32), V((NGY, 1, 128), F32), V((1, 128), F32), V((NGX, 1, 128), F32),
-        V((34, 8, 128), F32), DMA((8,)), DMA((7, 2)),
+        V((34, 8, 128), F32), DMA((8,)), DMA((8, 2)),
     ]
-    out = jax.ShapeDtypeStruct((3, 2, 2, 9), F32)
-    return pl.pallas_call(
+    both = pl.pallas_call(
         kernel,
-        out_shape=(out, out),
+        out_shape=jax.ShapeDtypeStruct((6, 2, 2, 9), F32),
         in_specs=[hbm] * 8,
-        out_specs=(vmem, vmem),
+        out_specs=vmem,
         scratch_shapes=scratch,
         compiler_params=pltpu.CompilerParams(
             collective_id=0, has_side_effects=True, vmem_limit_bytes=55210 * 1024
         ),
     )(reference_scan, deformed_scan, table, *consts)
+    return both[:3], both[3:]
 
 
 def solution(mesh):

time: 40.9 us -> 39.1 us (0.956)
  Pallas kernels: 38.9 us -> 37.8 us
  local copies, waits for them, and re-layouts: 1.19 us -> 0.6 us
    unnamed x2 -> x0, local copies, waits for them, and re-layouts: 1.19 us -> none
    pallas_call x1, Pallas kernels: 38.9 us -> 37.8 us  [local(): pl.pallas_call(kernel, out_shape=jax.ShapeDtypeStruct((6, 2, 2, 9), F32),...]
    slice x0 -> x1, local copies, waits for them, and re-layouts: none -> 0.6 us  [local(): return (both[:3], both[3:])]
where the time goes in v5:
time: 39.1 us; the launch traced here: 39 us
  Pallas kernels  37.8 us (97%)
  between operations  0.64 us (2%)
  local copies, waits for them, and re-layouts  0.6 us (2%)
    pallas_call x1, Pallas kernels, local(): pl.pallas_call(kernel, out_shape=jax.ShapeDtypeStruct((6, 2, 2, 9), F32),...  37.8 us

profile of v5, /device:TPU:1, one launch (start us, length us, event | category | flops | bytes accessed | tf_op | source)
XLA Modules:
  0.0 39.0 jit_solution(10058989005342306169)
XLA Ops:
  0.6 37.8 %shard_map.95 = f32[6,2,2,9]{3,2,1,0:T(2,128)S(1)} custom-call(bf16[32,32,128]{2,1,0:T(8,128)(2,1)} %ref_h.1, bf16[32,32,128]{2,1,0:T(8,128)(2,1)} %def_h.1, s32[32,1,64]{2,1,0:T(1,128)} %bitcast.1, bf16[80,192]{1,0:T(8,128)(2,1)} %constant.10.clone.ys_h, bf16[640,512]{1,0:T(8,128)(2,1)} %constant.11.clone.wmat_h, bf16[384,128]{1,0:T(8,128)(2,1)} %constant.12.clone.wr_h, ...), custom_call_target="tpu_custom_call" | custom-call | tf_op jit(solution)/shard_map/pallas_call | solution.py:631
  38.4 0.6 %fusion = (f32[3,2,2,9]{3,2,1,0:T(2,128)}, f32[3,2,2,9]{3,2,1,0:T(2,128)}) fusion(f32[6,2,2,9]{3,2,1,0:T(2,128)S(1)} %shard_map.95), kind=kLoop, calls=%fused_computation | loop fusion | bytes 1728 | tf_op jit(solution)/shard_map/slice | solution.py:641

commit v6 on v5

--- a/solution.py
+++ b/solution.py
@@ -13,6 +13,7 @@
 E = 16
 ITERS = 4
 DAMPING = 0.1
+KSCALE = 4.0
 NGX, NGY = 8, 32
 F32, BF16 = jnp.float32, jnp.bfloat16
 
@@ -43,7 +44,7 @@
 def constants():
     wy, cy = chain(32, 3)
     wz, cz = chain(128, 9)
-    scale = 1.0 / 1024.0
+    scale = 1.0 / (1024.0 * KSCALE)
     ymat = np.zeros((48, 192))
     for m in range(5):
         for p in range(6):
@@ -571,7 +572,8 @@
         return total
 
     one = jnp.ones_like(m0)
-    center = mu + DAMPING
+    center = KSCALE * mu + DAMPING
+    beside = KSCALE * spread_q
     residual = [one, None, None, None, None]
     direction = list(residual)
     update = [None] * 5
@@ -583,9 +585,9 @@
             if d is None:
                 continue
             image[k] = add(image[k], center * d)
-            image[k + 1] = add(image[k + 1], d)
+            image[k + 1] = add(image[k + 1], KSCALE * d)
             if k:
-                image[k - 1] = add(image[k - 1], spread_q * d)
+                image[k - 1] = add(image[k - 1], beside * d)
         alpha = rr / form(direction, image)
         update = [add(u, None if d is None else alpha * d) for u, d in zip(update, direction)]
         residual = [add(r, None if q is None else -(alpha * q)) for r, q in zip(residual, image)]

time: 39.1 us -> 39.1 us (level)
  no operation moved by 1% of the time
where the time goes in v6:
time: 39.1 us; the launch traced here: 39 us
  Pallas kernels  37.8 us (97%)
  between operations  0.64 us (2%)
  local copies, waits for them, and re-layouts  0.6 us (2%)
    pallas_call x1, Pallas kernels, local(): pl.pallas_call(kernel, out_shape=jax.ShapeDtypeStruct((6, 2, 2, 9), F32),...  37.8 us

profile of v6, /device:TPU:1, one launch (start us, length us, event | category | flops | bytes accessed | tf_op | source)
XLA Modules:
  0.0 39.0 jit_solution(9643445195519689066)
XLA Ops:
  0.6 37.8 %shard_map.95 = f32[6,2,2,9]{3,2,1,0:T(2,128)S(1)} custom-call(bf16[32,32,128]{2,1,0:T(8,128)(2,1)} %ref_h.1, bf16[32,32,128]{2,1,0:T(8,128)(2,1)} %def_h.1, s32[32,1,64]{2,1,0:T(1,128)} %bitcast.1, bf16[80,192]{1,0:T(8,128)(2,1)} %constant.10.clone.ys_h, bf16[640,512]{1,0:T(8,128)(2,1)} %constant.11.clone.wmat_h, bf16[384,128]{1,0:T(8,128)(2,1)} %constant.12.clone.wr_h, ...), custom_call_target="tpu_custom_call" | custom-call | tf_op jit(solution)/shard_map/pallas_call | solution.py:633
  38.4 0.6 %fusion = (f32[3,2,2,9]{3,2,1,0:T(2,128)}, f32[3,2,2,9]{3,2,1,0:T(2,128)}) fusion(f32[6,2,2,9]{3,2,1,0:T(2,128)S(1)} %shard_map.95), kind=kLoop, calls=%fused_computation | loop fusion | bytes 1728 | tf_op jit(solution)/shard_map/slice | solution.py:643
